TPU v7x, 1024 devices: a whole 8x8x8 slice. The times are simulated.
1024 devices in a mesh: row: 64 (over x, y), col: 16 (over z, core).
Axes of the slice: x: 8, y: 8, z: 8, core: 2. Of those that a mesh axis runs over, the one named last changes fastest.
Arguments:
- source_feats: bfloat16 [32768, 256], P(('col', 'row')), may hold values from -6 to 6
- target_feats: bfloat16 [131072, 256], P(('row', 'col')), may hold values from -6 to 6
- w_neigh: bfloat16 [256, 256], replicated, may hold values from -0.375 to 0.375
- w_self: bfloat16 [256, 256], replicated, may hold values from -0.375 to 0.375
- tile_count: int32 [64, 16], P('row', 'col'), may hold values from 1 to 48, as said below
- tile_rows: int32 [64, 16, 48], P('row', 'col'), may hold values from 0 to 15, as said below
- tile_cols: int32 [64, 16, 48], P('row', 'col'), may hold values from 0 to 15, as said below
- tile_vals: bfloat16 [64, 16, 48, 128, 128], P('row', 'col'), may hold values from -0.15625 to 0.15625
- cotangent: bfloat16 [131072, 256], P(('row', 'col')), may hold values from -6 to 6
Outputs:
- layer_out: bfloat16 [131072, 256], P(('row', 'col'))
- d_target: bfloat16 [131072, 256], P(('row', 'col'))
- d_source: bfloat16 [32768, 256], P(('col', 'row'))
- grad_neigh: float32 [256, 256], replicated
- grad_self: float32 [256, 256], replicated
Inputs may be any that keep to these rules, and one draw needn't show every extreme that they name: `tile_count`: every block has between 1 and 48 live slots, and some block has exactly 48. `tile_rows`: together with tile_cols, the slots of one block name distinct tile positions. `tile_cols`: together with tile_rows, the slots of one block name distinct tile positions.
All inputs are finite; a program needn't handle non-finite values.
Results may differ from a plain program's by a relative error of at most 0.0062.
Values may be sent and summed in bfloat16 or wider, within the bound.
No kernel may reach another device: no remote copies, remote signals or barrier semaphores. Data moves between devices by JAX's collectives and lax.ppermute only.
A program may use at most 64 MiB of HBM per device.

v0:
```python
import jax
import jax.numpy as jnp
from jax import lax
from jax.sharding import PartitionSpec as P

RB = 16
CB = 16


def gelu_parts(preact):
    normal_cdf = 0.5 * (1.0 + jax.scipy.special.erf(preact * 0.7071067811865476))
    density = jnp.exp(-0.5 * preact * preact) * 0.3989422804014327
    return (preact * normal_cdf, normal_cdf + preact * density)


def dense_step(aggregate, own_feats, cotangent, w_neigh, w_self):
    preact = jnp.dot(aggregate, w_neigh, preferred_element_type=jnp.float32) + jnp.dot(
        own_feats, w_self, preferred_element_type=jnp.float32
    )
    activated, slope = gelu_parts(preact)
    d_preact = (cotangent.astype(jnp.float32) * slope).astype(jnp.bfloat16)
    return (activated.astype(jnp.bfloat16), d_preact)


def on_device(
    source_feats,
    target_feats,
    w_neigh,
    w_self,
    tile_count,
    tile_rows,
    tile_cols,
    tile_vals,
    cotangent,
):
    width = source_feats.shape[1]
    values_here = tile_vals[0, 0]
    slot_count = values_here.shape[0]
    tile_size = values_here.shape[1]
    rows_here = tile_rows[0, 0]
    columns_here = tile_cols[0, 0]
    live_mask = (lax.iota(jnp.int32, slot_count) < tile_count[0, 0]).astype(jnp.float32)
    row_pick = (rows_here[:, None] == lax.iota(jnp.int32, RB)[None, :]).astype(
        jnp.float32
    ) * live_mask[:, None]
    col_pick = (columns_here[:, None] == lax.iota(jnp.int32, CB)[None, :]).astype(
        jnp.float32
    ) * live_mask[:, None]
    block_source = lax.all_gather(source_feats, "row", axis=0, tiled=True)
    source_tiles = block_source.reshape(CB, tile_size, width)[columns_here]
    products = jnp.einsum(
        "sij,sjf->sif", values_here, source_tiles, preferred_element_type=jnp.float32
    )
    partial_rows = jnp.einsum(
        "sr,sif->rif", row_pick, products, precision=lax.Precision.HIGHEST
    ).reshape(RB * tile_size, width)
    aggregate = lax.psum_scatter(partial_rows, "col", scatter_dimension=0, tiled=True).astype(
        jnp.bfloat16
    )
    layer_out, d_preact = dense_step(aggregate, target_feats, cotangent, w_neigh, w_self)
    d_own = jnp.dot(d_preact, w_neigh.T, preferred_element_type=jnp.float32).astype(jnp.bfloat16)
    d_aggregate = lax.all_gather(d_own, "col", axis=0, tiled=True)
    weight_grads = lax.psum(
        (
            jnp.dot(aggregate.T, d_preact, preferred_element_type=jnp.float32),
            jnp.dot(target_feats.T, d_preact, preferred_element_type=jnp.float32),
        ),
        ("row", "col"),
    )
    d_target = jnp.dot(d_preact, w_self.T, preferred_element_type=jnp.float32).astype(jnp.bfloat16)
    grad_tiles = d_aggregate.reshape(RB, tile_size, width)[rows_here]
    backward = jnp.einsum(
        "sji,sjf->sif", values_here, grad_tiles, preferred_element_type=jnp.float32
    )
    source_part = jnp.einsum(
        "sc,sif->cif", col_pick, backward, precision=lax.Precision.HIGHEST
    ).reshape(CB * tile_size, width)
    d_source = lax.psum_scatter(source_part, "row", scatter_dimension=0, tiled=True).astype(
        jnp.bfloat16
    )
    return (layer_out, d_target, d_source, weight_grads[0], weight_grads[1])


def solution(mesh):
    in_specs = (
        P(("col", "row"), None),
        P(("row", "col"), None),
        P(),
        P(),
        P("row", "col"),
        P("row", "col", None),
        P("row", "col", None),
        P("row", "col", None, None, None),
        P(("row", "col"), None),
    )
    out_specs = (
        P(("row", "col"), None),
        P(("row", "col"), None),
        P(("col", "row"), None),
        P(),
        P(),
    )
    return jax.shard_map(
        on_device, mesh=mesh, in_specs=in_specs, out_specs=out_specs, check_vma=False
    )
```

profile of v0, /device:TPU:1, one launch (start us, length us, event | category | flops | bytes accessed | tf_op | source)
XLA Modules:
  0.0 789.2 jit_solution(17842055103045888878)
XLA Ops:
  7.2 0.0 copy-start
  7.2 0.0 all-gather.3.cloned.1.call-start
  7.2 0.7 all-gather.3.cloned.1.call-update
  7.9 0.0 reduce-scatter.3.cloned.1.call-start
  8.6 0.7 fusion.28
  9.3 97.4 %all-gather.3.cloned.1.call-done = bf16[2048,256]{1,0:T(8,128)(2,1)} async-done(((bf16[32,256]{1,0:T(8,128)(2,1)}), bf16[2048,256]{1,0:T(8,128)(2,1)}) %all-gather.3.cloned.1.call-update) | async-done | bytes 1048592 | tf_op jit(solution)/shard_map/all_gather | solution.py:49
  106.7 3.8 gather_fusion
  110.5 0.0 copy-done
  110.5 5.6 fusion.6
  116.1 0.0 copy-start.4
  116.1 6.7 copy.18
  122.7 0.0 copy-done.4
  122.7 5.1 fusion.2
  127.9 0.0 copy-start.1
  127.9 0.0 copy-start.2
  127.9 0.0 copy-start.3
  127.9 0.0 copy-start.6
  127.9 2.5 copy.15
  130.5 0.0 reduce-scatter.3.cloned.1.call-update
  130.5 0.0 all-gather.5.cloned.1.call-start
  130.6 66.6 %reduce-scatter.3.cloned.1.call-done = f32[128,256]{1,0:T(8,128)} async-done(((f32[2048,256]{1,0:T(8,128)}), f32[128,256]{1,0:T(8,128)}) %reduce-scatter.3.cloned.1.call-update) | async-done | bytes 131088 | tf_op jit(solution)/shard_map/reduce_scatter | solution.py:57
  197.2 0.0 copy-done.1
  197.2 1.1 fusion.16
  198.3 0.0 copy-done.2
  198.3 0.0 copy-done.3
  198.3 0.0 copy-done.6
  198.3 0.9 fusion.13
  199.2 0.8 convolution_convert_fusion
  200.0 0.0 all-gather.5.cloned.1.call-update
  200.0 0.0 all-reduce.3.cloned.1.call-start
  200.1 0.9 convolution_bitcast_fusion
  201.0 1.8 fusion.14
  202.8 0.0 all-reduce.3.cloned.1.call-update
  202.8 0.0 reduce-scatter.5.cloned.1.call-start
  202.9 44.0 %all-gather.5.cloned.1.call-done = bf16[2048,256]{1,0:T(8,128)(2,1)} async-done(((bf16[128,256]{1,0:T(8,128)(2,1)}), bf16[2048,256]{1,0:T(8,128)(2,1)}) %all-gather.5.cloned.1.call-update) | async-done | bytes 1048592 | tf_op jit(solution)/shard_map/all_gather | solution.py:62
  246.9 3.8 gather_fusion.1
  250.7 5.6 fusion.4
  256.3 6.7 copy.19
  263.0 0.0 copy-done.5
  263.0 5.1 fusion
  268.1 2.5 copy.16
  270.7 0.0 reduce-scatter.5.cloned.1.call-update
  270.7 0.8 convolution_convert_fusion.1
  271.5 265.1 %all-reduce.3.cloned.1.call-done = (f32[256,256]{1,0:T(8,128)}, f32[256,256]{0,1:T(8,128)}) async-done(((f32[256,256]{1,0:T(8,128)}, f32[256,256]{0,1:T(8,128)}), (f32[256,256]{1,0:T(8,128)}, f32[256,256]{0,1:T(8,128)})) %all-reduce.3.cloned.1.call-update) | async-done | bytes 524304 | tf_op jit(solution)/shard_map/psum | solution.py:63
  536.6 1.8 copy.17
  538.4 241.2 %reduce-scatter.5.cloned.1.call-done = f32[32,256]{1,0:T(8,128)} async-done(((f32[2048,256]{1,0:T(8,128)}), f32[32,256]{1,0:T(8,128)}) %reduce-scatter.5.cloned.1.call-update) | async-done | bytes 32784 | tf_op jit(solution)/shard_map/reduce_scatter | solution.py:78
  779.6 1.4 convert_element_type.37
  781.0 1.7 copy.23
  (5 shorter events, 0.0 us)
Async XLA Ops:
  7.2 103.3 %copy-start = (bf16[1,1,48,128,128]{4,3,2,1,0:T(8,128)(2,1)S(1)}, bf16[1,1,48,128,128]{4,3,2,1,0:T(8,128)(2,1)}, u32[]{:S(2)}) copy-start(bf16[1,1,48,128,128]{4,3,2,1,0:T(8,128)(2,1)} %param.16) | copy-start | bytes 4718596
  7.2 99.5 %all-gather.3.cloned.1.call-start = ((), (), s32[]{:S(2)}) async-start(), calls=%async_computation.2 | async-start | bytes 1064960 | tf_op jit(solution)/shard_map/all_gather | solution.py:49
  7.9 189.3 %reduce-scatter.3.cloned.1.call-start = ((), (), s32[]{:S(2)}) async-start(), calls=%async_computation.3 | async-start | bytes 2228224 | tf_op jit(solution)/shard_map/reduce_scatter | solution.py:57
  116.1 6.7 copy-start.4
  127.9 69.3 %copy-start.1 = (bf16[256,256]{1,0:T(8,128)(2,1)S(1)}, bf16[256,256]{1,0:T(8,128)(2,1)}, u32[]{:S(2)}) copy-start(bf16[256,256]{1,0:T(8,128)(2,1)} %param.11) | copy-start | bytes 393220
  127.9 70.4 %copy-start.2 = (bf16[256,256]{1,0:T(8,128)(2,1)S(1)}, bf16[256,256]{1,0:T(8,128)(2,1)}, u32[]{:S(2)}) copy-start(bf16[256,256]{1,0:T(8,128)(2,1)} %param.12) | copy-start | bytes 393220
  127.9 70.4 %copy-start.3 = (bf16[128,256]{1,0:T(8,128)(2,1)S(1)}, bf16[128,256]{1,0:T(8,128)(2,1)}, u32[]{:S(2)}) copy-start(bf16[128,256]{1,0:T(8,128)(2,1)} %param.10) | copy-start | bytes 196612
  127.9 70.4 %copy-start.6 = (bf16[128,256]{1,0:T(8,128)(2,1)S(1)}, bf16[128,256]{1,0:T(8,128)(2,1)}, u32[]{:S(2)}) copy-start(bf16[128,256]{1,0:T(8,128)(2,1)} %param.17) | copy-start | bytes 196612
  130.5 116.4 %all-gather.5.cloned.1.call-start = ((), (), s32[]{:S(2)}) async-start(), calls=%async_computation.4 | async-start | bytes 1114112 | tf_op jit(solution)/shard_map/all_gather | solution.py:62
  200.0 336.6 %all-reduce.3.cloned.1.call-start = ((), (), s32[]{:S(2)}) async-start(), calls=%async_computation.6 | async-start | bytes 1048576 | tf_op jit(solution)/shard_map/psum | solution.py:63
  202.8 576.8 %reduce-scatter.5.cloned.1.call-start = ((), (), s32[]{:S(2)}) async-start(), calls=%async_computation.5 | async-start | bytes 2129920 | tf_op jit(solution)/shard_map/reduce_scatter | solution.py:78
  256.3 6.7 copy-start.5
Sparse Core Ops, SparseCore 0:
  12.2 94.4 all-gather.2
  130.6 66.5 reduce-scatter.2
  200.5 46.3 all-gather.4
  252.3 284.2 all-reduce.2
  542.5 237.0 reduce-scatter.4
where the time goes:
time: 794 us; the launch traced here: 789 us
  waiting for transfers between devices  715 us (90%)
  local copies, waits for them, and re-layouts  29.5 us (4%)
  matrix products  27.7 us (3%)
  between operations  14.5 us (2%)
    psum x1, waiting for transfers between devices, on_device(): lax.psum((jnp.dot(aggregate.T, d_preact, preferred_element_type=jnp.float...  265 us
    reduce_scatter x1, waiting for transfers between devices, on_device(): lax.psum_scatter(source_part, 'row', scatter_dimension=0, tiled=True)  241 us
    all_gather x1, waiting for transfers between devices, on_device(): block_source = lax.all_gather(source_feats, 'row', axis=0, tiled=True)  97.4 us
    reduce_scatter x1, waiting for transfers between devices, on_device(): lax.psum_scatter(partial_rows, 'col', scatter_dimension=0, tiled=True)  66.6 us
    all_gather x1, waiting for transfers between devices, on_device(): d_aggregate = lax.all_gather(d_own, 'col', axis=0, tiled=True)  44 us
  transfers between devices with their start and end apart: 5, of which 5 were waited for; matrix products, arithmetic and copies ran while one was open for 4% of the time, Pallas kernels for 0%

commit v1 on v0

v1 whole, which is shorter than its diff:
```python
import jax
import jax.numpy as jnp
from jax import lax
from jax.experimental import pallas as pl
from jax.experimental.pallas import tpu as pltpu
from jax.sharding import PartitionSpec as P

RB = 16
CB = 16
TILE = 128
GROUP = 4
F32 = jnp.float32
BF16 = jnp.bfloat16
VMEM = pl.BlockSpec(memory_space=pltpu.VMEM)
SMEM = pl.BlockSpec(memory_space=pltpu.SMEM)
PARAMS = pltpu.CompilerParams(vmem_limit_bytes=32 * 1024 * 1024)


def live_groups(count_ref):
    return (count_ref[0, 0] + (GROUP - 1)) // GROUP


def forward_tiles(count_ref, rows_ref, cols_ref, vals_ref, src_ref, out_ref, total):
    count = count_ref[0, 0]
    total[...] = jnp.zeros_like(total)

    def group(g, carry):
        for k in range(GROUP):
            s = g * GROUP + k
            at = pl.ds(pl.multiple_of(rows_ref[0, 0, s] * TILE, TILE), TILE)
            of = pl.ds(pl.multiple_of(cols_ref[0, 0, s] * TILE, TILE), TILE)
            product = jnp.dot(vals_ref[0, 0, s], src_ref[of, :], preferred_element_type=F32)
            total[at, :] += jnp.where(s < count, product, 0.0)
        return carry

    lax.fori_loop(0, live_groups(count_ref), group, 0)
    out_ref[...] = total[...].astype(BF16)


def backward_tiles(
    count_ref, rows_ref, cols_ref, vals_ref, d_pre_ref, w_neigh_ref, out_ref, d_agg, total
):
    count = count_ref[0, 0]
    total[...] = jnp.zeros_like(total)
    d_agg[...] = lax.dot_general(
        d_pre_ref[...], w_neigh_ref[...], (((1,), (1,)), ((), ())), preferred_element_type=F32
    ).astype(BF16)

    def group(g, carry):
        for k in range(GROUP):
            s = g * GROUP + k
            of = pl.ds(pl.multiple_of(rows_ref[0, 0, s] * TILE, TILE), TILE)
            at = pl.ds(pl.multiple_of(cols_ref[0, 0, s] * TILE, TILE), TILE)
            product = lax.dot_general(
                vals_ref[0, 0, s], d_agg[of, :], (((0,), (0,)), ((), ())), preferred_element_type=F32
            )
            total[at, :] += jnp.where(s < count, product, 0.0)
        return carry

    lax.fori_loop(0, live_groups(count_ref), group, 0)
    out_ref[...] = total[...].astype(BF16)


def dense_step(
    parts_ref, own_ref, cot_ref, w_neigh_ref, w_self_ref, out_ref, d_tgt_ref, d_pre_ref, feats_ref
):
    agg = jnp.sum(parts_ref[...].astype(F32), axis=0).astype(BF16)
    own = own_ref[...]
    preact = jnp.dot(agg, w_neigh_ref[...], preferred_element_type=F32) + jnp.dot(
        own, w_self_ref[...], preferred_element_type=F32
    )
    cdf = 0.5 * (1.0 + lax.erf(preact * 0.7071067811865476))
    density = jnp.exp(-0.5 * preact * preact) * 0.3989422804014327
    out_ref[...] = (preact * cdf).astype(BF16)
    d_pre = (cot_ref[...].astype(F32) * (cdf + preact * density)).astype(BF16)
    d_pre_ref[...] = d_pre
    d_tgt_ref[...] = lax.dot_general(
        d_pre, w_self_ref[...], (((1,), (1,)), ((), ())), preferred_element_type=F32
    ).astype(BF16)
    width = own.shape[1]
    feats_ref[:width, :] = agg.T
    feats_ref[width:, :] = own.T


def grad_step(feats_ref, d_pre_ref, out_ref):
    n, rows, _ = feats_ref.shape
    total = jnp.zeros(out_ref.shape, F32)
    for k in range(n):
        total += jnp.dot(
            feats_ref[k], d_pre_ref[k * TILE : (k + 1) * TILE, :], preferred_element_type=F32
        )
    out_ref[...] = total


def sum_step(parts_ref, out_ref):
    out_ref[...] = jnp.sum(parts_ref[...].astype(F32), axis=0).astype(BF16)


def call(kernel, ins, outs, scratch=()):
    single = not isinstance(outs, list)
    return pl.pallas_call(
        kernel,
        out_shape=outs,
        in_specs=ins,
        out_specs=VMEM if single else [VMEM] * len(outs),
        scratch_shapes=scratch,
        compiler_params=PARAMS,
    )


def on_device(
    source_feats, target_feats, w_neigh, w_self, tile_count, tile_rows, tile_cols, tile_vals, cotangent
):
    width = source_feats.shape[1]
    n_col = lax.axis_size("col")
    n_row = lax.axis_size("row")
    own_rows = target_feats.shape[0]
    sds = jax.ShapeDtypeStruct
    slots = [SMEM, SMEM, SMEM, VMEM]

    block_source = lax.all_gather(source_feats, "row", axis=0, tiled=True)
    partial_rows = call(
        forward_tiles, slots + [VMEM], sds((RB * TILE, width), BF16),
        [pltpu.VMEM((RB * TILE, width), F32)],
    )(tile_count, tile_rows, tile_cols, tile_vals, block_source)
    parts = lax.all_to_all(partial_rows, "col", 0, 0, tiled=True)
    layer_out, d_target, d_preact, feats = call(
        dense_step, [VMEM] * 5,
        [sds((own_rows, width), BF16)] * 3 + [sds((2 * width, own_rows), BF16)],
    )(parts.reshape(n_col, own_rows, width), target_feats, cotangent, w_neigh, w_self)

    d_pre_block = lax.all_gather(d_preact, "col", axis=0, tiled=True)
    share = width // n_col
    feats = feats.reshape(2, n_col, share, own_rows).swapaxes(0, 1).reshape(2 * width, own_rows)
    feat_parts = lax.all_to_all(feats, "col", 0, 0, tiled=True)
    grads = call(grad_step, [VMEM] * 2, sds((2 * share, width), F32))(
        feat_parts.reshape(n_col, 2 * share, own_rows), d_pre_block
    )
    source_part = call(
        backward_tiles, slots + [VMEM, VMEM], sds((CB * TILE, width), BF16),
        [pltpu.VMEM((RB * TILE, width), BF16), pltpu.VMEM((CB * TILE, width), F32)],
    )(tile_count, tile_rows, tile_cols, tile_vals, d_pre_block, w_neigh)
    source_parts = lax.all_to_all(source_part, "row", 0, 0, tiled=True)
    d_source = call(sum_step, [VMEM], sds(source_feats.shape, BF16))(
        source_parts.reshape(n_row, -1, width)
    )
    grads = lax.psum(grads, "row")
    grads = lax.all_gather(grads, "col", axis=0, tiled=False)
    grads = grads.reshape(n_col, 2, share, width).swapaxes(0, 1).reshape(2, width, width)
    return (layer_out, d_target, d_source, grads[0], grads[1])


def solution(mesh):
    in_specs = (
        P(("col", "row"), None),
        P(("row", "col"), None),
        P(),
        P(),
        P("row", "col"),
        P("row", "col", None),
        P("row", "col", None),
        P("row", "col", None, None, None),
        P(("row", "col"), None),
    )
    out_specs = (
        P(("row", "col"), None),
        P(("row", "col"), None),
        P(("col", "row"), None),
        P(),
        P(),
    )
    return jax.shard_map(
        on_device, mesh=mesh, in_specs=in_specs, out_specs=out_specs, check_vma=False
    )
```

time: 794 us -> 533 us (0.67)
  waiting for transfers between devices: 715 us -> 135 us
  blocking collectives: 0 us -> 353 us
  matrix products: 27.7 us -> 0 us
  local copies, waits for them, and re-layouts: 29.5 us -> 6.7 us
  starting transfers between devices: 0.2 us -> 15.9 us
    reduce_scatter x2 -> x0, waiting for transfers between devices: 308 us -> none  [the longest x1 241 us: on_device(): lax.psum_scatter(source_part, 'row', scatter_dimension=0, tiled=True)]
    psum x1 -> x0, waiting for transfers between devices: 265 us -> none  [on_device(): lax.psum((jnp.dot(aggregate.T, d_preact, preferred_element_type=jnp.float...]
    psum x0 -> x1, blocking collectives: none -> 239 us  [on_device(): grads = lax.psum(grads, 'row')]
    all_gather x0 -> x1, blocking collectives: none -> 73 us  [on_device(): grads = lax.all_gather(grads, 'col', axis=0, tiled=False)]
    all_to_all x0 -> x1, blocking collectives: none -> 41 us  [on_device(): parts = lax.all_to_all(partial_rows, 'col', 0, 0, tiled=True)]
    dot_general x10 -> x0, matrix products: 27.7 us -> none  [the longest x1 5.58 us: on_device(): jnp.einsum('sij,sjf->sif', values_here, source_tiles, preferred_element_t...]
    dot_general x4 -> x0, local copies, waits for them, and re-layouts: 18.5 us -> none  [the longest x1 6.68 us: on_device(): jnp.einsum('sij,sjf->sif', values_here, source_tiles, preferred_element_t...]
    all_to_all x0 -> x2, starting transfers between devices: none -> 15.8 us  [the longest x1 12.4 us: on_device(): source_parts = lax.all_to_all(source_part, 'row', 0, 0, tiled=True)]
  transfers between devices with their start and end apart: 5 -> 4, of which waited for: 5 -> 2; matrix products, arithmetic and copies ran while one was open for 4% -> 0% of each run, Pallas kernels for 0% -> 1%
where the time goes in v1:
time: 533 us; the launch traced here: 532 us
  blocking collectives  353 us (66%)
  waiting for transfers between devices  135 us (25%)
  starting transfers between devices  15.9 us (3%)
  between operations  14.8 us (3%)
  Pallas kernels  7 us (1%)
  local copies, waits for them, and re-layouts  6.7 us (1%)
    psum x1, blocking collectives, on_device(): grads = lax.psum(grads, 'row')  239 us
    all_gather x1, waiting for transfers between devices, on_device(): block_source = lax.all_gather(source_feats, 'row', axis=0, tiled=True)  98.1 us
    all_gather x1, blocking collectives, on_device(): grads = lax.all_gather(grads, 'col', axis=0, tiled=False)  73 us
    all_to_all x1, blocking collectives, on_device(): parts = lax.all_to_all(partial_rows, 'col', 0, 0, tiled=True)  41 us
    all_gather x1, waiting for transfers between devices, on_device(): d_pre_block = lax.all_gather(d_preact, 'col', axis=0, tiled=True)  36 us
    all_to_all x1, starting transfers between devices, on_device(): source_parts = lax.all_to_all(source_part, 'row', 0, 0, tiled=True)  12.4 us
  transfers between devices with their start and end apart: 4, of which 2 were waited for; matrix products, arithmetic and copies ran while one was open for 0% of the time, Pallas kernels for 1%

profile of v1, /device:TPU:1, one launch (start us, length us, event | category | flops | bytes accessed | tf_op | source)
XLA Modules:
  0.0 532.0 jit_solution(9878626658409354519)
XLA Ops:
  7.2 0.0 all-gather.3.cloned.1.call-start
  7.2 0.7 all-gather.3.cloned.1.call-update
  7.9 0.0 all-gather.5.cloned.1.call-start
  8.6 98.1 %all-gather.3.cloned.1.call-done.src_ref = bf16[2048,256]{1,0:T(8,128)(2,1)} async-done(((bf16[32,256]{1,0:T(8,128)(2,1)}), bf16[2048,256]{1,0:T(8,128)(2,1)}) %all-gather.3.cloned.1.call-update) | async-done | bytes 1048592 | tf_op jit(solution)/shard_map/all_gather | solution.py:121
  106.7 0.0 copy-start
  106.7 1.4 copy-done
  108.1 0.0 copy-start.4
  108.1 1.2 copy-done.4
  109.3 0.0 copy-start.9
  109.3 0.7 copy-done.9
  110.0 0.0 copy-start.11
  110.0 0.7 copy-done.11
  110.6 1.7 shard_map.128
  112.3 0.0 copy-start.5
  112.3 0.0 copy-start.6
  112.4 0.0 copy-start.7
  112.4 0.0 copy-start.8
  112.4 0.0 copy-start.1
  112.4 0.0 copy-start.10
  112.4 0.0 copy-start.12
  112.4 41.0 %all_to_all.27.parts_ref = bf16[16,128,256]{2,1,0:T(8,128)(2,1)S(1)} all-to-all(bf16[16,128,256]{2,1,0:T(8,128)(2,1)S(1)} %bitcast.12), channel_id=1, replica_groups=mesh['row'=64,'col'=16] {'col'}, dimensions={0} | all-to-all | bytes 2097152 | tf_op jit(solution)/shard_map/all_to_all | solution.py:126
  153.5 0.0 copy-done.5
  153.5 0.0 copy-done.6
  153.5 0.0 copy-done.7
  153.5 0.0 copy-done.8
  153.5 1.1 shard_map.129
  154.6 0.0 all-gather.5.cloned.1.call-update
  154.6 0.7 copy.15
  155.2 3.4 all-to-all-start.2
  158.7 36.0 %all-gather.5.cloned.1.call-done.d_pre_ref = bf16[2048,256]{1,0:T(8,128)(2,1)} async-done(((bf16[128,256]{1,0:T(8,128)(2,1)}), bf16[2048,256]{1,0:T(8,128)(2,1)}) %all-gather.5.cloned.1.call-update) | async-done | bytes 1048592 | tf_op jit(solution)/shard_map/all_gather | solution.py:132
  194.6 0.0 copy-done.1
  194.6 0.0 copy-done.10
  194.7 0.0 copy-done.12
  194.7 0.0 copy-start.2
  194.7 1.2 copy-done.2
  195.9 3.2 shard_map.130
  199.1 0.0 copy-start.3
  199.1 0.0 all-to-all-done.2.feats_ref
  199.1 12.4 %all-to-all-start.1 = ((bf16[64,32,256]{2,1,0:T(8,128)(2,1)}), bf16[64,32,256]{2,1,0:T(8,128)(2,1)S(1)}, u32[]{:S(2)}, u32[]{:S(2)}) async-start(bf16[64,32,256]{2,1,0:T(8,128)(2,1)} %bitcast.1), calls=%async_computation.1 | async-start | bytes 2097152 | tf_op jit(solution)/shard_map/all_to_all | solution.py:143
  211.5 0.0 copy-done.3
  211.5 0.3 shard_map.132
  211.8 238.9 %psum.7 = f32[1,32,256]{2,1,0:T(8,128)S(1)} all-reduce(f32[1,32,256]{2,1,0:T(8,128)S(1)} %bitcast.13), channel_id=1, replica_groups=mesh['row'=64,'col'=16] {'row'}, use_global_device_ids=true, to_apply=%region_0.0 | all-reduce | flops 8192 | bytes 65536 | tf_op jit(solution)/shard_map/psum | solution.py:147
  450.6 73.0 %all_gather.15 = f32[16,32,256]{2,1,0:T(8,128)S(1)} all-gather(f32[1,32,256]{2,1,0:T(8,128)S(1)} %psum.7), channel_id=1, replica_groups=mesh['row'=64,'col'=16] {'col'}, dimensions={0}, use_global_device_ids=true | all-gather | bytes 557056 | tf_op jit(solution)/shard_map/all_gather | solution.py:148
  523.6 0.8 fusion
  524.4 0.0 all-to-all-done.1.parts_ref
  524.4 0.8 shard_map.131
Async XLA Ops:
  7.2 99.5 %all-gather.3.cloned.1.call-start = ((), (), s32[]{:S(2)}) async-start(), calls=%async_computation.3 | async-start | bytes 1064960 | tf_op jit(solution)/shard_map/all_gather | solution.py:121
  7.9 186.7 %all-gather.5.cloned.1.call-start = ((), (), s32[]{:S(2)}) async-start(), calls=%async_computation.4 | async-start | bytes 1114112 | tf_op jit(solution)/shard_map/all_gather | solution.py:132
  106.7 1.4 copy-start
  108.1 1.2 copy-start.4
  109.3 0.7 copy-start.9
  110.0 0.7 copy-start.11
  112.3 41.1 %copy-start.5 = (bf16[256,256]{1,0:T(8,128)(2,1)S(1)}, bf16[256,256]{1,0:T(8,128)(2,1)}, u32[]{:S(2)}) copy-start(bf16[256,256]{1,0:T(8,128)(2,1)} %w_neigh_ref.3) | copy-start | bytes 393220
  112.3 41.1 %copy-start.6 = (bf16[256,256]{1,0:T(8,128)(2,1)S(1)}, bf16[256,256]{1,0:T(8,128)(2,1)}, u32[]{:S(2)}) copy-start(bf16[256,256]{1,0:T(8,128)(2,1)} %w_self_ref.1) | copy-start | bytes 393220
  112.4 41.1 %copy-start.7 = (bf16[128,256]{1,0:T(8,128)(2,1)S(1)}, bf16[128,256]{1,0:T(8,128)(2,1)}, u32[]{:S(2)}) copy-start(bf16[128,256]{1,0:T(8,128)(2,1)} %own_ref.1) | copy-start | bytes 196612
  112.4 41.1 %copy-start.8 = (bf16[128,256]{1,0:T(8,128)(2,1)S(1)}, bf16[128,256]{1,0:T(8,128)(2,1)}, u32[]{:S(2)}) copy-start(bf16[128,256]{1,0:T(8,128)(2,1)} %cot_ref.1) | copy-start | bytes 196612
  112.4 82.3 %copy-start.1 = (bf16[1,1,48,128,128]{4,3,2,1,0:T(8,128)(2,1)S(1)}, bf16[1,1,48,128,128]{4,3,2,1,0:T(8,128)(2,1)}, u32[]{:S(2)}) copy-start(bf16[1,1,48,128,128]{4,3,2,1,0:T(8,128)(2,1)} %vals_ref.3) | copy-start | bytes 4718596
  112.4 82.3 %copy-start.10 = (s32[1,1,48]{2,1,0:T(1,128)S(1)}, s32[1,1,48]{2,1,0:T(1,128)}, u32[]{:S(2)}) copy-start(s32[1,1,48]{2,1,0:T(1,128)} %rows_ref.3) | copy-start | bytes 580
  112.4 82.3 %copy-start.12 = (s32[1,1,48]{2,1,0:T(1,128)S(1)}, s32[1,1,48]{2,1,0:T(1,128)}, u32[]{:S(2)}) copy-start(s32[1,1,48]{2,1,0:T(1,128)} %cols_ref.3) | copy-start | bytes 580
  155.2 43.8 %all-to-all-start.2 = ((bf16[16,32,128]{2,1,0:T(8,128)(2,1)}), bf16[16,32,128]{2,1,0:T(8,128)(2,1)S(1)}, u32[]{:S(2)}, u32[]{:S(2)}) async-start(bf16[16,32,128]{2,1,0:T(8,128)(2,1)} %bitcast.4), calls=%async_computation.2 | async-start | bytes 262144 | tf_op jit(solution)/shard_map/all_to_all | solution.py:135
  194.7 1.2 copy-start.2
  199.1 12.4 %copy-start.3 = (bf16[2048,256]{1,0:T(8,128)(2,1)S(1)}, bf16[2048,256]{1,0:T(8,128)(2,1)}, u32[]{:S(2)}) copy-start(bf16[2048,256]{1,0:T(8,128)(2,1)} %all-gather.5.cloned.1.call-done.d_pre_ref) | copy-start | bytes 3145732
  199.1 325.4 %all-to-all-start.1 = ((bf16[64,32,256]{2,1,0:T(8,128)(2,1)}), bf16[64,32,256]{2,1,0:T(8,128)(2,1)S(1)}, u32[]{:S(2)}, u32[]{:S(2)}) async-start(bf16[64,32,256]{2,1,0:T(8,128)(2,1)} %bitcast.1), calls=%async_computation.1 | async-start | bytes 2097152 | tf_op jit(solution)/shard_map/all_to_all | solution.py:143
Sparse Core Ops, SparseCore 0:
  12.2 94.4 all-gather.2
  154.7 39.8 all-gather.4

commit v2 on v1

v2 whole, which is shorter than its diff:
```python
import jax
import jax.numpy as jnp
from jax import lax
from jax.experimental import pallas as pl
from jax.experimental.pallas import tpu as pltpu
from jax.sharding import Mesh, PartitionSpec as P

RB = 16
CB = 16
TILE = 128
GROUP = 4
SHARE = 16
TAIL = 16
ROW = ("x", "y")
COL = ("z", "core")
F32 = jnp.float32
BF16 = jnp.bfloat16
VMEM = pl.BlockSpec(memory_space=pltpu.VMEM)
SMEM = pl.BlockSpec(memory_space=pltpu.SMEM)
PARAMS = pltpu.CompilerParams(vmem_limit_bytes=32 * 1024 * 1024)


def live_groups(count_ref):
    return (count_ref[0, 0] + (GROUP - 1)) // GROUP


def forward_tiles(
    core_ref, count_ref, rows_ref, cols_ref, vals_ref, src_ref, mine_ref, send_ref, total
):
    count = count_ref[0, 0]
    total[...] = jnp.zeros_like(total)

    def group(g, carry):
        for k in range(GROUP):
            s = g * GROUP + k
            at = pl.ds(pl.multiple_of(rows_ref[0, 0, s] * TILE, TILE), TILE)
            of = pl.ds(pl.multiple_of(cols_ref[0, 0, s] * TILE, TILE), TILE)
            product = jnp.dot(vals_ref[0, 0, s], src_ref[of, :], preferred_element_type=F32)
            total[at, :] += jnp.where(s < count, product, 0.0)
        return carry

    lax.fori_loop(0, live_groups(count_ref), group, 0)
    core = core_ref[0, 0]
    share = mine_ref.shape[0] // (RB // 2)
    for k in range(RB // 2):
        here = slice(k * share, (k + 1) * share)
        keep = pl.ds(pl.multiple_of((2 * k + core) * share, share), share)
        give = pl.ds(pl.multiple_of((2 * k + 1 - core) * share, share), share)
        mine_ref[here, :] = total[keep, :]
        send_ref[here, :] = total[give, :].astype(BF16)


def assemble(head_ref, swap_ref, d_pre):
    n = swap_ref.shape[0]
    head = head_ref.shape[0] // n
    full = head + TAIL
    half = d_pre.shape[1] // 2
    for k in range(n):
        d_pre[k * full : k * full + head, :] = head_ref[k * head : (k + 1) * head, :]
        rows = slice(k * full + head, (k + 1) * full)
        d_pre[rows, :half] = swap_ref[k, 2 * SHARE : 2 * SHARE + TAIL, :]
        d_pre[rows, half:] = swap_ref[k, 2 * SHARE + TAIL : 2 * SHARE + 2 * TAIL, :]


def backward_tiles(
    count_ref, rows_ref, cols_ref, vals_ref, head_ref, swap_ref, w_neigh_ref, out_ref,
    d_pre, d_agg, total,
):
    count = count_ref[0, 0]
    total[...] = jnp.zeros_like(total)
    assemble(head_ref, swap_ref, d_pre)
    d_agg[...] = lax.dot_general(
        d_pre[...], w_neigh_ref[...], (((1,), (1,)), ((), ())), preferred_element_type=F32
    ).astype(BF16)

    def group(g, carry):
        for k in range(GROUP):
            s = g * GROUP + k
            of = pl.ds(pl.multiple_of(rows_ref[0, 0, s] * TILE, TILE), TILE)
            at = pl.ds(pl.multiple_of(cols_ref[0, 0, s] * TILE, TILE), TILE)
            product = lax.dot_general(
                vals_ref[0, 0, s], d_agg[of, :], (((0,), (0,)), ((), ())), preferred_element_type=F32
            )
            total[at, :] += jnp.where(s < count, product, 0.0)
        return carry

    lax.fori_loop(0, live_groups(count_ref), group, 0)
    out_ref[...] = total[...].astype(BF16)


def dense_step(
    parts_ref, own_ref, cot_ref, w_neigh_ref, w_self_ref, out_ref, d_tgt_ref, head_ref, swap_ref
):
    agg = jnp.sum(parts_ref[...].astype(F32), axis=0).astype(BF16)
    own = own_ref[...]
    preact = jnp.dot(agg, w_neigh_ref[...], preferred_element_type=F32) + jnp.dot(
        own, w_self_ref[...], preferred_element_type=F32
    )
    cdf = 0.5 * (1.0 + lax.erf(preact * 0.7071067811865476))
    density = jnp.exp(-0.5 * preact * preact) * 0.3989422804014327
    out_ref[...] = (preact * cdf).astype(BF16)
    d_pre = (cot_ref[...].astype(F32) * (cdf + preact * density)).astype(BF16)
    d_tgt_ref[...] = lax.dot_general(
        d_pre, w_self_ref[...], (((1,), (1,)), ((), ())), preferred_element_type=F32
    ).astype(BF16)
    head = head_ref.shape[0]
    half = d_pre.shape[1] // 2
    head_ref[...] = d_pre[:head, :]
    agg_t = agg.T
    own_t = own.T
    for k in range(swap_ref.shape[0]):
        swap_ref[k, :SHARE, :] = agg_t[k * SHARE : (k + 1) * SHARE, :]
        swap_ref[k, SHARE : 2 * SHARE, :] = own_t[k * SHARE : (k + 1) * SHARE, :]
        swap_ref[k, 2 * SHARE : 2 * SHARE + TAIL, :] = d_pre[head:, :half]
        swap_ref[k, 2 * SHARE + TAIL :, :] = d_pre[head:, half:]


def grad_step(head_ref, swap_ref, out_ref, d_pre):
    assemble(head_ref, swap_ref, d_pre)
    n = swap_ref.shape[0]
    total = jnp.zeros((2 * SHARE, d_pre.shape[1]), F32)
    for k in range(n):
        total += jnp.dot(
            swap_ref[k, : 2 * SHARE, :], d_pre[k * TILE : (k + 1) * TILE, :],
            preferred_element_type=F32,
        )
    out_ref[...] = total


def sum_step(parts_ref, out_ref):
    out_ref[...] = jnp.sum(parts_ref[...].astype(F32), axis=0).astype(BF16)


def call(kernel, ins, outs, scratch=()):
    single = not isinstance(outs, list)
    return pl.pallas_call(
        kernel,
        out_shape=outs,
        in_specs=ins,
        out_specs=VMEM if single else [VMEM] * len(outs),
        scratch_shapes=scratch,
        compiler_params=PARAMS,
    )


def on_device(
    source_feats, target_feats, w_neigh, w_self, tile_count, tile_rows, tile_cols, tile_vals, cotangent
):
    width = source_feats.shape[1]
    n_x, n_y, n_z = (lax.axis_size(a) for a in ("x", "y", "z"))
    n_col = lax.axis_size(COL)
    n_row = lax.axis_size(ROW)
    own_rows = target_feats.shape[0]
    own_source = source_feats.shape[0]
    sds = jax.ShapeDtypeStruct
    slots = [SMEM, SMEM, SMEM, VMEM]
    rows = RB * TILE

    block_source = lax.all_to_all(
        jnp.broadcast_to(source_feats[None], (n_row, own_source, width)), ROW, 0, 0, tiled=True
    ).reshape(rows, width)
    core = lax.axis_index("core").astype(jnp.int32).reshape(1, 1)
    mine, send = call(
        forward_tiles, [SMEM] + slots + [VMEM],
        [sds((rows // 2, width), F32), sds((rows // 2, width), BF16)],
        [pltpu.VMEM((rows, width), F32)],
    )(core, tile_count, tile_rows, tile_cols, tile_vals, block_source)
    got = lax.ppermute(send, "core", [(0, 1), (1, 0)])
    pair = (mine + got.astype(F32)).astype(BF16)
    parts = lax.all_to_all(pair, "z", 0, 0, tiled=True)
    layer_out, d_target, head, swap = call(
        dense_step, [VMEM] * 5,
        [sds((own_rows, width), BF16)] * 2
        + [sds((own_rows - TAIL, width), BF16), sds((n_col, 2 * SHARE + 2 * TAIL, own_rows), BF16)],
    )(parts.reshape(n_z, own_rows, width), target_feats, cotangent, w_neigh, w_self)

    swapped = lax.all_to_all(swap, COL, 0, 0, tiled=True)
    heads = lax.all_gather(head, COL, axis=0, tiled=True)
    grads = call(
        grad_step, [VMEM] * 2, sds((2 * SHARE, width), F32),
        [pltpu.VMEM((rows, width), BF16)],
    )(heads, swapped)
    grads_y = lax.all_to_all(
        jnp.broadcast_to(grads[None], (n_y,) + grads.shape), "y", 0, 0, tiled=True
    )
    source_part = call(
        backward_tiles, slots + [VMEM] * 3, sds((CB * TILE, width), BF16),
        [pltpu.VMEM((rows, width), BF16)] * 2 + [pltpu.VMEM((CB * TILE, width), F32)],
    )(tile_count, tile_rows, tile_cols, tile_vals, heads, swapped, w_neigh)
    source_parts = lax.all_to_all(source_part, ROW, 0, 0, tiled=True)
    grads = jnp.sum(grads_y, axis=0)
    grads_x = lax.all_gather(grads, ("x", "core"), axis=0, tiled=False)
    grads_x = grads_x.reshape((n_x, 2) + grads.shape)
    grads = jnp.sum(lax.dynamic_index_in_dim(grads_x, core[0, 0], 1, keepdims=False), axis=0)
    all_grads = lax.all_gather(grads, COL, axis=0, tiled=False)
    d_source = call(sum_step, [VMEM], sds(source_feats.shape, BF16))(
        source_parts.reshape(n_row, -1, width)
    )
    all_grads = all_grads.reshape(n_col, 2, SHARE, width).swapaxes(0, 1).reshape(2, width, width)
    return (layer_out, d_target, d_source, all_grads[0], all_grads[1])


def solution(mesh):
    n_row, n_col = mesh.devices.shape
    n_y = min(n_row, 8)
    mesh = Mesh(mesh.devices.reshape(n_row // n_y, n_y, n_col // 2, 2), ROW + COL)
    targets = P(ROW + COL, None)
    sources = P(COL + ROW, None)
    in_specs = (
        sources,
        targets,
        P(),
        P(),
        P(ROW, COL),
        P(ROW, COL, None),
        P(ROW, COL, None),
        P(ROW, COL, None, None, None),
        targets,
    )
    out_specs = (targets, targets, sources, P(), P())
    return jax.shard_map(
        on_device, mesh=mesh, in_specs=in_specs, out_specs=out_specs, check_vma=False
    )
```

time: 533 us -> 194 us (0.36)
  blocking collectives: 353 us -> 110 us
  waiting for transfers between devices: 135 us -> 31.9 us
  starting transfers between devices: 15.9 us -> 38.1 us
  between operations: 14.8 us -> 1.38 us
    psum x1 -> x0, blocking collectives: 239 us -> none  [on_device(): grads = lax.psum(grads, 'row')]
    all_gather x2 -> x0, waiting for transfers between devices: 134 us -> none  [the longest x1 98.1 us: on_device(): block_source = lax.all_gather(source_feats, 'row', axis=0, tiled=True)]
    all_to_all x2 -> x4, waiting for transfers between devices: 0.01 us -> 30.3 us  [the longest x1 22.1 us: on_device(): lax.all_to_all(jnp.broadcast_to(source_feats[None], (n_row, own_source, w...]
    all_to_all x2 -> x4, starting transfers between devices: 15.8 us -> 29.3 us  [the longest x1 14 us: on_device(): lax.all_to_all(jnp.broadcast_to(source_feats[None], (n_row, own_source, w...]
    ppermute x0 -> x1, starting transfers between devices: none -> 8.8 us  [on_device(): got = lax.ppermute(send, 'core', [(0, 1), (1, 0)])]
    all_to_all x1, blocking collectives: 41 us -> 32.7 us  [on_device(): parts = lax.all_to_all(pair, 'z', 0, 0, tiled=True)]
    all_gather x1 -> x3, blocking collectives: 73 us -> 77 us  [the longest x1 37.8 us: on_device(): grads_x = lax.all_gather(grads, ('x', 'core'), axis=0, tiled=False)]
  transfers between devices with their start and end apart: 4 -> 5, of which waited for: 2 -> 3; matrix products, arithmetic and copies ran while one was open for 0% -> 0% of each run, Pallas kernels for 1% -> 2%
where the time goes in v2:
time: 194 us; the launch traced here: 193 us
  blocking collectives  110 us (57%)
  starting transfers between devices  38.1 us (20%)
  waiting for transfers between devices  31.9 us (16%)
  Pallas kernels  8.66 us (4%)
  local copies, waits for them, and re-layouts  3.52 us (2%)
    all_gather x1, blocking collectives, on_device(): grads_x = lax.all_gather(grads, ('x', 'core'), axis=0, tiled=False)  37.8 us
    all_to_all x1, blocking collectives, on_device(): parts = lax.all_to_all(pair, 'z', 0, 0, tiled=True)  32.7 us
    all_gather x1, blocking collectives, on_device(): heads = lax.all_gather(head, COL, axis=0, tiled=True)  23.1 us
    all_to_all x1, waiting for transfers between devices, on_device(): lax.all_to_all(jnp.broadcast_to(source_feats[None], (n_row, own_source, w...  22.1 us
    all_gather x1, blocking collectives, on_device(): all_grads = lax.all_gather(grads, COL, axis=0, tiled=False)  16 us
    all_to_all x1, starting transfers between devices, on_device(): lax.all_to_all(jnp.broadcast_to(source_feats[None], (n_row, own_source, w...  14 us
    ppermute x1, starting transfers between devices, on_device(): got = lax.ppermute(send, 'core', [(0, 1), (1, 0)])  8.8 us
    all_to_all x1, waiting for transfers between devices, on_device(): lax.all_to_all(jnp.broadcast_to(grads[None], (n_y,) + grads.shape), 'y',...  8.19 us
  transfers between devices with their start and end apart: 5, of which 3 were waited for; matrix products, arithmetic and copies ran while one was open for 0% of the time, Pallas kernels for 2%

profile of v2, /device:TPU:1, one launch (start us, length us, event | category | flops | bytes accessed | tf_op | source)
XLA Modules:
  0.0 193.3 jit_solution(13912990093854606074)
XLA Ops:
  0.6 0.0 copy-start
  0.6 0.0 copy-start.6
  0.7 0.0 copy-start.5
  0.7 1.9 broadcast_in_dim.4
  2.6 14.0 %all-to-all-start = ((bf16[64,32,256]{2,1,0:T(8,128)(2,1)}), bf16[64,32,256]{2,1,0:T(8,128)(2,1)S(1)}, u32[]{:S(2)}, u32[]{:S(2)}) async-start(bf16[64,32,256]{2,1,0:T(8,128)(2,1)} %broadcast_in_dim.4), calls=%async_computation | async-start | bytes 2097152 | tf_op jit(solution)/shard_map/all_to_all | solution.py:159
  17.3 22.1 %all-to-all-done = bf16[64,32,256]{2,1,0:T(8,128)(2,1)S(1)} async-done(((bf16[64,32,256]{2,1,0:T(8,128)(2,1)}), bf16[64,32,256]{2,1,0:T(8,128)(2,1)S(1)}, u32[]{:S(2)}, u32[]{:S(2)}) %all-to-all-start) | async-done | bytes 1048608 | tf_op jit(solution)/shard_map/all_to_all | solution.py:159
  39.4 0.0 copy-done
  39.4 0.0 copy-done.6
  39.4 0.0 copy-done.5
  39.4 2.4 %shard_map.128 = (f32[1024,256]{1,0:T(8,128)S(1)}, bf16[1024,256]{1,0:T(8,128)(2,1)S(1)}) custom-call(s32[1,1]{1,0:T(1,128)} %bitcast.core_ref, s32[1,1]{1,0:T(1,128)S(6)} %copy.14.count_ref, s32[1,1,48]{2,1,0:T(1,128)S(1)} %copy-done.5, s32[1,1,48]{2,1,0:T(1,128)S(1)} %copy-done.6, bf16[1,1,48,128,128]{4,3,2,1,0:T(8,128)(2,1)S(1)} %copy-done, ...), custom_call_target="tpu_custom_call" | custom-call | tf_op jit(solution)/shard_map/pallas_call | solution.py:163
  41.9 8.8 %collective-permute-start = (bf16[1024,256]{1,0:T(8,128)(2,1)S(1)}, bf16[1024,256]{1,0:T(8,128)(2,1)S(1)}, u32[]{:S(2)}, u32[]{:S(2)}) collective-permute-start(bf16[1024,256]{1,0:T(8,128)(2,1)S(1)} %get-tuple-element.12), channel_id=1, source_target_pairs={{0,1},{1,0},{2,3},{3,2},{4,5},{5,4},{6,7},{7,6},{8,9},{9,8},{10,11... | collective-permute-start | bytes 1572872 | tf_op jit(solution)/shard_map/ppermute | solution.py:168
  50.7 1.5 collective-permute-done
  52.2 0.0 copy-start.1
  52.2 0.0 copy-start.2
  52.2 0.0 copy-start.3
  52.2 0.0 copy-start.4
  52.2 0.1 add_convert_fusion
  52.3 32.7 %all_to_all.33.parts_ref = bf16[8,128,256]{2,1,0:T(8,128)(2,1)S(1)} all-to-all(bf16[8,128,256]{2,1,0:T(8,128)(2,1)S(1)} %bitcast.12), channel_id=1, replica_groups=mesh['x'=8,'y'=8,'z'=8,'core'=2] {'z'}, dimensions={0} | all-to-all | bytes 1048576 | tf_op jit(solution)/shard_map/all_to_all | solution.py:170
  85.1 0.0 copy-done.1
  85.1 0.0 copy-done.2
  85.1 0.0 copy-done.3
  85.1 0.0 copy-done.4
  85.1 1.1 shard_map.129
  86.2 5.1 %all-to-all-start.2 = ((bf16[16,64,128]{2,1,0:T(8,128)(2,1)}), bf16[16,64,128]{2,1,0:T(8,128)(2,1)S(1)}, u32[]{:S(2)}, u32[]{:S(2)}) async-start(bf16[16,64,128]{2,1,0:T(8,128)(2,1)} %get-tuple-element.16), calls=%async_computation.2 | async-start | bytes 524288 | tf_op jit(solution)/shard_map/all_to_all | solution.py:177
  91.3 23.1 %all_gather.15.head_ref = bf16[1792,256]{1,0:T(8,128)(2,1)S(1)} all-gather(bf16[112,256]{1,0:T(8,128)(2,1)S(1)} %get-tuple-element.15), channel_id=1, replica_groups=mesh['x'=8,'y'=8,'z'=8,'core'=2] {'z','core'}, dimensions={0}, use_global_device_ids=true | all-gather | bytes 974848 | tf_op jit(solution)/shard_map/all_gather | solution.py:178
  114.4 0.0 all-to-all-done.2.swap_ref
  114.5 0.3 shard_map.132
  114.7 0.7 broadcast_in_dim.5
  115.5 5.5 %all-to-all-start.4 = ((f32[8,32,256]{2,1,0:T(8,128)}), f32[8,32,256]{2,1,0:T(8,128)S(1)}, u32[]{:S(2)}, u32[]{:S(2)}) async-start(f32[8,32,256]{2,1,0:T(8,128)} %broadcast_in_dim.5), calls=%async_computation.4 | async-start | bytes 524288 | tf_op jit(solution)/shard_map/all_to_all | solution.py:183
  120.9 4.1 %shard_map.130 = bf16[2048,256]{1,0:T(8,128)(2,1)} custom-call(s32[1,1]{1,0:T(1,128)S(6)} %copy.14.count_ref, s32[1,1,48]{2,1,0:T(1,128)S(1)} %copy-done.5, s32[1,1,48]{2,1,0:T(1,128)S(1)} %copy-done.6, bf16[1,1,48,128,128]{4,3,2,1,0:T(8,128)(2,1)S(1)} %copy-done, bf16[1792,256]{1,0:T(8,128)(2,1)S(1)} %all_gather.15.head_ref, ...), custom_call_target="tpu_custom_call" | custom-call | tf_op jit(solution)/shard_map/pallas_call | solution.py:186
  125.0 8.2 %all-to-all-done.4 = f32[8,32,256]{2,1,0:T(8,128)S(1)} async-done(((f32[8,32,256]{2,1,0:T(8,128)}), f32[8,32,256]{2,1,0:T(8,128)S(1)}, u32[]{:S(2)}, u32[]{:S(2)}) %all-to-all-start.4) | async-done | bytes 262176 | tf_op jit(solution)/shard_map/all_to_all | solution.py:183
  133.2 4.7 %all-to-all-start.3 = ((bf16[64,32,256]{2,1,0:T(8,128)(2,1)}), bf16[64,32,256]{2,1,0:T(8,128)(2,1)S(1)}, u32[]{:S(2)}, u32[]{:S(2)}) async-start(bf16[64,32,256]{2,1,0:T(8,128)(2,1)} %bitcast.3), calls=%async_computation.3 | async-start | bytes 2097152 | tf_op jit(solution)/shard_map/all_to_all | solution.py:190
  137.9 37.8 %all-gather = f32[512,256]{1,0:T(8,128)S(1)} all-gather(f32[32,256]{1,0:T(8,128)S(1)} %reduce_sum.18), channel_id=2, replica_groups=mesh['x'=8,'y'=8,'z'=8,'core'=2] {'x','core'}, dimensions={0}, use_global_device_ids=true | all-gather | bytes 557056 | tf_op jit(solution)/shard_map/all_gather | solution.py:192
  175.7 16.0 %all-gather.1 = f32[512,256]{1,0:T(8,128)S(1)} all-gather(f32[32,256]{1,0:T(8,128)S(1)} %dynamic-slice_reduce_fusion), channel_id=3, replica_groups=mesh['x'=8,'y'=8,'z'=8,'core'=2] {'z','core'}, dimensions={0}, use_global_device_ids=true | all-gather | bytes 557056 | tf_op jit(solution)/shard_map/all_gather | solution.py:195
  191.7 0.8 fusion
  192.6 0.0 all-to-all-done.3.parts_ref
  192.6 0.8 shard_map.131
  (2 shorter events, 0.0 us)
Async XLA Ops:
  0.6 38.8 %copy-start = (bf16[1,1,48,128,128]{4,3,2,1,0:T(8,128)(2,1)S(1)}, bf16[1,1,48,128,128]{4,3,2,1,0:T(8,128)(2,1)}, u32[]{:S(2)}) copy-start(bf16[1,1,48,128,128]{4,3,2,1,0:T(8,128)(2,1)} %vals_ref.3) | copy-start | bytes 4718596
  0.6 38.8 %copy-start.6 = (s32[1,1,48]{2,1,0:T(1,128)S(1)}, s32[1,1,48]{2,1,0:T(1,128)}, u32[]{:S(2)}) copy-start(s32[1,1,48]{2,1,0:T(1,128)} %cols_ref.3) | copy-start | bytes 580
  0.7 38.8 %copy-start.5 = (s32[1,1,48]{2,1,0:T(1,128)S(1)}, s32[1,1,48]{2,1,0:T(1,128)}, u32[]{:S(2)}) copy-start(s32[1,1,48]{2,1,0:T(1,128)} %rows_ref.3) | copy-start | bytes 580
  2.6 36.8 %all-to-all-start = ((bf16[64,32,256]{2,1,0:T(8,128)(2,1)}), bf16[64,32,256]{2,1,0:T(8,128)(2,1)S(1)}, u32[]{:S(2)}, u32[]{:S(2)}) async-start(bf16[64,32,256]{2,1,0:T(8,128)(2,1)} %broadcast_in_dim.4), calls=%async_computation | async-start | bytes 2097152 | tf_op jit(solution)/shard_map/all_to_all | solution.py:159
  41.9 10.3 %collective-permute-start = (bf16[1024,256]{1,0:T(8,128)(2,1)S(1)}, bf16[1024,256]{1,0:T(8,128)(2,1)S(1)}, u32[]{:S(2)}, u32[]{:S(2)}) collective-permute-start(bf16[1024,256]{1,0:T(8,128)(2,1)S(1)} %get-tuple-element.12), channel_id=1, source_target_pairs={{0,1},{1,0},{2,3},{3,2},{4,5},{5,4},{6,7},{7,6},{8,9},{9,8},{10,11... | collective-permute-start | bytes 1572872 | tf_op jit(solution)/shard_map/ppermute | solution.py:168
  52.2 32.9 %copy-start.1 = (bf16[256,256]{1,0:T(8,128)(2,1)S(1)}, bf16[256,256]{1,0:T(8,128)(2,1)}, u32[]{:S(2)}) copy-start(bf16[256,256]{1,0:T(8,128)(2,1)} %w_neigh_ref.3) | copy-start | bytes 393220
  52.2 32.9 %copy-start.2 = (bf16[256,256]{1,0:T(8,128)(2,1)S(1)}, bf16[256,256]{1,0:T(8,128)(2,1)}, u32[]{:S(2)}) copy-start(bf16[256,256]{1,0:T(8,128)(2,1)} %w_self_ref.1) | copy-start | bytes 393220
  52.2 32.9 %copy-start.3 = (bf16[128,256]{1,0:T(8,128)(2,1)S(1)}, bf16[128,256]{1,0:T(8,128)(2,1)}, u32[]{:S(2)}) copy-start(bf16[128,256]{1,0:T(8,128)(2,1)} %own_ref.1) | copy-start | bytes 196612
  52.2 32.9 %copy-start.4 = (bf16[128,256]{1,0:T(8,128)(2,1)S(1)}, bf16[128,256]{1,0:T(8,128)(2,1)}, u32[]{:S(2)}) copy-start(bf16[128,256]{1,0:T(8,128)(2,1)} %cot_ref.1) | copy-start | bytes 196612
  86.2 28.3 %all-to-all-start.2 = ((bf16[16,64,128]{2,1,0:T(8,128)(2,1)}), bf16[16,64,128]{2,1,0:T(8,128)(2,1)S(1)}, u32[]{:S(2)}, u32[]{:S(2)}) async-start(bf16[16,64,128]{2,1,0:T(8,128)(2,1)} %get-tuple-element.16), calls=%async_computation.2 | async-start | bytes 524288 | tf_op jit(solution)/shard_map/all_to_all | solution.py:177
  115.5 17.7 %all-to-all-start.4 = ((f32[8,32,256]{2,1,0:T(8,128)}), f32[8,32,256]{2,1,0:T(8,128)S(1)}, u32[]{:S(2)}, u32[]{:S(2)}) async-start(f32[8,32,256]{2,1,0:T(8,128)} %broadcast_in_dim.5), calls=%async_computation.4 | async-start | bytes 524288 | tf_op jit(solution)/shard_map/all_to_all | solution.py:183
  133.2 59.4 %all-to-all-start.3 = ((bf16[64,32,256]{2,1,0:T(8,128)(2,1)}), bf16[64,32,256]{2,1,0:T(8,128)(2,1)S(1)}, u32[]{:S(2)}, u32[]{:S(2)}) async-start(bf16[64,32,256]{2,1,0:T(8,128)(2,1)} %bitcast.3), calls=%async_computation.3 | async-start | bytes 2097152 | tf_op jit(solution)/shard_map/all_to_all | solution.py:190

commit v3 on v2

--- a/solution.py
+++ b/solution.py
@@ -63,7 +63,7 @@
 
 
 def backward_tiles(
-    count_ref, rows_ref, cols_ref, vals_ref, head_ref, swap_ref, w_neigh_ref, out_ref,
+    count_ref, rows_ref, cols_ref, vals_ref, head_ref, swap_ref, w_neigh_ref, after_ref, out_ref,
     d_pre, d_agg, total,
 ):
     count = count_ref[0, 0]
@@ -124,7 +124,20 @@
             swap_ref[k, : 2 * SHARE, :], d_pre[k * TILE : (k + 1) * TILE, :],
             preferred_element_type=F32,
         )
-    out_ref[...] = total
+    for k in range(out_ref.shape[0]):
+        out_ref[k] = total
+
+
+def repeat_step(one_ref, out_ref):
+    one = one_ref[...]
+    for k in range(out_ref.shape[0]):
+        out_ref[k] = one
+
+
+def sum_repeat_step(parts_ref, out_ref):
+    total = jnp.sum(parts_ref[...], axis=0)
+    for k in range(out_ref.shape[0]):
+        out_ref[k] = total
 
 
 def sum_step(parts_ref, out_ref):
@@ -157,7 +170,8 @@
     rows = RB * TILE
 
     block_source = lax.all_to_all(
-        jnp.broadcast_to(source_feats[None], (n_row, own_source, width)), ROW, 0, 0, tiled=True
+        call(repeat_step, [VMEM], sds((n_row, own_source, width), BF16))(source_feats),
+        ROW, 0, 0, tiled=True,
     ).reshape(rows, width)
     core = lax.axis_index("core").astype(jnp.int32).reshape(1, 1)
     mine, send = call(
@@ -177,21 +191,18 @@
     swapped = lax.all_to_all(swap, COL, 0, 0, tiled=True)
     heads = lax.all_gather(head, COL, axis=0, tiled=True)
     grads = call(
-        grad_step, [VMEM] * 2, sds((2 * SHARE, width), F32),
+        grad_step, [VMEM] * 2, sds((n_y, 2 * SHARE, width), F32),
         [pltpu.VMEM((rows, width), BF16)],
     )(heads, swapped)
-    grads_y = lax.all_to_all(
-        jnp.broadcast_to(grads[None], (n_y,) + grads.shape), "y", 0, 0, tiled=True
-    )
+    grads = lax.all_to_all(grads, "y", 0, 0, tiled=True)
+    grads = call(sum_repeat_step, [VMEM], sds((n_x, 2 * SHARE, width), F32))(grads)
+    grads_x = lax.all_to_all(grads, "x", 0, 0, tiled=True)
     source_part = call(
-        backward_tiles, slots + [VMEM] * 3, sds((CB * TILE, width), BF16),
+        backward_tiles, slots + [VMEM] * 3 + [pl.BlockSpec(memory_space=pl.ANY)], sds((CB * TILE, width), BF16),
         [pltpu.VMEM((rows, width), BF16)] * 2 + [pltpu.VMEM((CB * TILE, width), F32)],
-    )(tile_count, tile_rows, tile_cols, tile_vals, heads, swapped, w_neigh)
+    )(tile_count, tile_rows, tile_cols, tile_vals, heads, swapped, w_neigh, grads)
     source_parts = lax.all_to_all(source_part, ROW, 0, 0, tiled=True)
-    grads = jnp.sum(grads_y, axis=0)
-    grads_x = lax.all_gather(grads, ("x", "core"), axis=0, tiled=False)
-    grads_x = grads_x.reshape((n_x, 2) + grads.shape)
-    grads = jnp.sum(lax.dynamic_index_in_dim(grads_x, core[0, 0], 1, keepdims=False), axis=0)
+    grads = jnp.sum(grads_x, axis=0)
     all_grads = lax.all_gather(grads, COL, axis=0, tiled=False)
     d_source = call(sum_step, [VMEM], sds(source_feats.shape, BF16))(
         source_parts.reshape(n_row, -1, width)

time: 194 us -> 183 us (0.943)
  the two profiles are of different devices: /device:TPU:1 before, /device:TPU:4 now
where the time goes in v3:
time: 183 us; the launch traced here: 182 us
  blocking collectives  88.7 us (48%)
  waiting for transfers between devices  46.2 us (25%)
  starting transfers between devices  35.6 us (19%)
  Pallas kernels  7.5 us (4%)
  local copies, waits for them, and re-layouts  2.66 us (1%)
    all_to_all x1, blocking collectives, on_device(): parts = lax.all_to_all(pair, 'z', 0, 0, tiled=True)  34.4 us
    all_to_all x1, waiting for transfers between devices, on_device(): lax.all_to_all(call(repeat_step, [VMEM], sds((n_row, own_source, width),...  26 us
    all_gather x1, blocking collectives, on_device(): heads = lax.all_gather(head, COL, axis=0, tiled=True)  23.1 us
    all_to_all x1, starting transfers between devices, on_device(): lax.all_to_all(call(repeat_step, [VMEM], sds((n_row, own_source, width),...  17.3 us
    all_gather x1, blocking collectives, on_device(): all_grads = lax.all_gather(grads, COL, axis=0, tiled=False)  16 us
    all_to_all x1, blocking collectives, on_device(): grads = lax.all_to_all(grads, 'y', 0, 0, tiled=True)  15.1 us
    all_to_all x1, waiting for transfers between devices, on_device(): source_parts = lax.all_to_all(source_part, ROW, 0, 0, tiled=True)  12.2 us
    all_to_all x1, starting transfers between devices, on_device(): source_parts = lax.all_to_all(source_part, ROW, 0, 0, tiled=True)  7.16 us
  transfers between devices with their start and end apart: 5, of which 4 were waited for; matrix products, arithmetic and copies ran while one was open for 0% of the time, Pallas kernels for 2%

profile of v3, /device:TPU:4, one launch (start us, length us, event | category | flops | bytes accessed | tf_op | source)
XLA Modules:
  0.0 182.1 jit_solution(1326648670225378375)
XLA Ops:
  0.6 0.0 copy-start
  0.6 0.0 copy-start.6
  0.7 0.8 copy-done.6
  1.5 0.0 copy-start.7
  1.5 0.0 copy-start.8
  1.5 0.1 shard_map.128
  1.6 0.0 copy-start.1
  1.6 1.0 copy-done.1
  2.6 17.3 %all-to-all-start = ((bf16[64,32,256]{2,1,0:T(8,128)(2,1)}), bf16[64,32,256]{2,1,0:T(8,128)(2,1)S(1)}, u32[]{:S(2)}, u32[]{:S(2)}) async-start(bf16[64,32,256]{2,1,0:T(8,128)(2,1)} %copy-done.1), calls=%async_computation | async-start | bytes 2097152 | tf_op jit(solution)/shard_map/all_to_all | solution.py:172
  20.6 26.0 %all-to-all-done = bf16[64,32,256]{2,1,0:T(8,128)(2,1)S(1)} async-done(((bf16[64,32,256]{2,1,0:T(8,128)(2,1)}), bf16[64,32,256]{2,1,0:T(8,128)(2,1)S(1)}, u32[]{:S(2)}, u32[]{:S(2)}) %all-to-all-start) | async-done | bytes 1048608 | tf_op jit(solution)/shard_map/all_to_all | solution.py:172
  46.6 0.0 copy-done
  46.6 0.0 copy-done.7
  46.6 0.0 copy-done.8
  46.7 1.5 shard_map.129
  48.2 1.9 %collective-permute-start = (bf16[1024,256]{1,0:T(8,128)(2,1)S(1)}, bf16[1024,256]{1,0:T(8,128)(2,1)S(1)}, u32[]{:S(2)}, u32[]{:S(2)}) collective-permute-start(bf16[1024,256]{1,0:T(8,128)(2,1)S(1)} %get-tuple-element.12), channel_id=1, source_target_pairs={{0,1},{1,0},{2,3},{3,2},{4,5},{5,4},{6,7},{7,6},{8,9},{9,8},{10,11... | collective-permute-start | bytes 1572872 | tf_op jit(solution)/shard_map/ppermute | solution.py:182
  50.1 1.9 %collective-permute-done = bf16[1024,256]{1,0:T(8,128)(2,1)S(1)} collective-permute-done((bf16[1024,256]{1,0:T(8,128)(2,1)S(1)}, bf16[1024,256]{1,0:T(8,128)(2,1)S(1)}, u32[]{:S(2)}, u32[]{:S(2)}) %collective-permute-start) | collective-permute-done | bytes 524320 | tf_op jit(solution)/shard_map/ppermute | solution.py:182
  52.0 0.0 copy-start.2
  52.0 0.0 copy-start.3
  52.0 0.0 copy-start.4
  52.0 0.0 copy-start.5
  52.0 0.1 add_convert_fusion
  52.1 34.4 %all_to_all.38.parts_ref = bf16[8,128,256]{2,1,0:T(8,128)(2,1)S(1)} all-to-all(bf16[8,128,256]{2,1,0:T(8,128)(2,1)S(1)} %bitcast.11), channel_id=1, replica_groups=mesh['x'=8,'y'=8,'z'=8,'core'=2] {'z'}, dimensions={0} | all-to-all | bytes 1048576 | tf_op jit(solution)/shard_map/all_to_all | solution.py:184
  86.5 0.0 copy-done.2
  86.5 0.0 copy-done.3
  86.5 0.0 copy-done.4
  86.5 0.0 copy-done.5
  86.5 1.1 shard_map.130
  87.6 3.5 %all-to-all-start.2 = ((bf16[16,64,128]{2,1,0:T(8,128)(2,1)}), bf16[16,64,128]{2,1,0:T(8,128)(2,1)S(1)}, u32[]{:S(2)}, u32[]{:S(2)}) async-start(bf16[16,64,128]{2,1,0:T(8,128)(2,1)} %get-tuple-element.16), calls=%async_computation.2 | async-start | bytes 524288 | tf_op jit(solution)/shard_map/all_to_all | solution.py:191
  91.2 23.1 %all_gather.9.head_ref = bf16[1792,256]{1,0:T(8,128)(2,1)S(1)} all-gather(bf16[112,256]{1,0:T(8,128)(2,1)S(1)} %get-tuple-element.15), channel_id=1, replica_groups=mesh['x'=8,'y'=8,'z'=8,'core'=2] {'z','core'}, dimensions={0}, use_global_device_ids=true | all-gather | bytes 974848 | tf_op jit(solution)/shard_map/all_gather | solution.py:192
  114.2 0.0 all-to-all-done.2.swap_ref
  114.3 0.3 shard_map.131
  114.5 15.1 %all_to_all.39.parts_ref = f32[8,32,256]{2,1,0:T(8,128)S(1)} all-to-all(f32[8,32,256]{2,1,0:T(8,128)S(1)} %shard_map.131), channel_id=1, replica_groups=mesh['x'=8,'y'=8,'z'=8,'core'=2] {'y'}, dimensions={0} | all-to-all | bytes 524288 | tf_op jit(solution)/shard_map/all_to_all | solution.py:197
  129.7 0.7 shard_map.132.after_ref
  130.4 5.6 %all-to-all-start.5 = ((f32[8,32,256]{2,1,0:T(8,128)}), f32[8,32,256]{2,1,0:T(8,128)S(1)}, u32[]{:S(2)}, u32[]{:S(2)}) async-start(f32[8,32,256]{2,1,0:T(8,128)} %shard_map.132.after_ref), calls=%async_computation.5 | async-start | bytes 524288 | tf_op jit(solution)/shard_map/all_to_all | solution.py:199
  136.0 3.0 %shard_map.133 = bf16[2048,256]{1,0:T(8,128)(2,1)} custom-call(s32[1,1]{1,0:T(1,128)S(6)} %copy.14.count_ref, s32[1,1,48]{2,1,0:T(1,128)S(1)} %copy-done.7, s32[1,1,48]{2,1,0:T(1,128)S(1)} %copy-done.8, bf16[1,1,48,128,128]{4,3,2,1,0:T(8,128)(2,1)S(1)} %copy-done, bf16[1792,256]{1,0:T(8,128)(2,1)S(1)} %all_gather.9.head_ref, ...), custom_call_target="tpu_custom_call" | custom-call | tf_op jit(solution)/shard_map/pallas_call | solution.py:200
  139.0 6.0 %all-to-all-done.5 = f32[8,32,256]{2,1,0:T(8,128)S(1)} async-done(((f32[8,32,256]{2,1,0:T(8,128)}), f32[8,32,256]{2,1,0:T(8,128)S(1)}, u32[]{:S(2)}, u32[]{:S(2)}) %all-to-all-start.5) | async-done | bytes 262176 | tf_op jit(solution)/shard_map/all_to_all | solution.py:199
  145.0 7.2 %all-to-all-start.4 = ((bf16[64,32,256]{2,1,0:T(8,128)(2,1)}), bf16[64,32,256]{2,1,0:T(8,128)(2,1)S(1)}, u32[]{:S(2)}, u32[]{:S(2)}) async-start(bf16[64,32,256]{2,1,0:T(8,128)(2,1)} %bitcast.3), calls=%async_computation.4 | async-start | bytes 2097152 | tf_op jit(solution)/shard_map/all_to_all | solution.py:204
  152.2 16.0 %all-gather = f32[512,256]{1,0:T(8,128)S(1)} all-gather(f32[32,256]{1,0:T(8,128)S(1)} %reduce_sum.9), channel_id=2, replica_groups=mesh['x'=8,'y'=8,'z'=8,'core'=2] {'z','core'}, dimensions={0}, use_global_device_ids=true | all-gather | bytes 557056 | tf_op jit(solution)/shard_map/all_gather | solution.py:206
  168.3 0.8 fusion
  169.1 12.2 %all-to-all-done.4.parts_ref = bf16[64,32,256]{2,1,0:T(8,128)(2,1)S(1)} async-done(((bf16[64,32,256]{2,1,0:T(8,128)(2,1)}), bf16[64,32,256]{2,1,0:T(8,128)(2,1)S(1)}, u32[]{:S(2)}, u32[]{:S(2)}) %all-to-all-start.4) | async-done | bytes 1048608 | tf_op jit(solution)/shard_map/all_to_all | solution.py:204
  181.3 0.8 shard_map.134
  (1 shorter events, 0.0 us)
Async XLA Ops:
  0.6 46.0 %copy-start = (bf16[1,1,48,128,128]{4,3,2,1,0:T(8,128)(2,1)S(1)}, bf16[1,1,48,128,128]{4,3,2,1,0:T(8,128)(2,1)}, u32[]{:S(2)}) copy-start(bf16[1,1,48,128,128]{4,3,2,1,0:T(8,128)(2,1)} %vals_ref.3) | copy-start | bytes 4718596
  0.6 0.8 copy-start.6
  1.5 45.2 %copy-start.7 = (s32[1,1,48]{2,1,0:T(1,128)S(1)}, s32[1,1,48]{2,1,0:T(1,128)}, u32[]{:S(2)}) copy-start(s32[1,1,48]{2,1,0:T(1,128)} %rows_ref.3) | copy-start | bytes 580
  1.5 45.2 %copy-start.8 = (s32[1,1,48]{2,1,0:T(1,128)S(1)}, s32[1,1,48]{2,1,0:T(1,128)}, u32[]{:S(2)}) copy-start(s32[1,1,48]{2,1,0:T(1,128)} %cols_ref.3) | copy-start | bytes 580
  1.6 1.0 copy-start.1
  2.6 44.0 %all-to-all-start = ((bf16[64,32,256]{2,1,0:T(8,128)(2,1)}), bf16[64,32,256]{2,1,0:T(8,128)(2,1)S(1)}, u32[]{:S(2)}, u32[]{:S(2)}) async-start(bf16[64,32,256]{2,1,0:T(8,128)(2,1)} %copy-done.1), calls=%async_computation | async-start | bytes 2097152 | tf_op jit(solution)/shard_map/all_to_all | solution.py:172
  48.2 3.8 %collective-permute-start = (bf16[1024,256]{1,0:T(8,128)(2,1)S(1)}, bf16[1024,256]{1,0:T(8,128)(2,1)S(1)}, u32[]{:S(2)}, u32[]{:S(2)}) collective-permute-start(bf16[1024,256]{1,0:T(8,128)(2,1)S(1)} %get-tuple-element.12), channel_id=1, source_target_pairs={{0,1},{1,0},{2,3},{3,2},{4,5},{5,4},{6,7},{7,6},{8,9},{9,8},{10,11... | collective-permute-start | bytes 1572872 | tf_op jit(solution)/shard_map/ppermute | solution.py:182
  52.0 34.5 %copy-start.2 = (bf16[256,256]{1,0:T(8,128)(2,1)S(1)}, bf16[256,256]{1,0:T(8,128)(2,1)}, u32[]{:S(2)}) copy-start(bf16[256,256]{1,0:T(8,128)(2,1)} %w_neigh_ref.3) | copy-start | bytes 393220
  52.0 34.5 %copy-start.3 = (bf16[256,256]{1,0:T(8,128)(2,1)S(1)}, bf16[256,256]{1,0:T(8,128)(2,1)}, u32[]{:S(2)}) copy-start(bf16[256,256]{1,0:T(8,128)(2,1)} %w_self_ref.1) | copy-start | bytes 393220
  52.0 34.5 %copy-start.4 = (bf16[128,256]{1,0:T(8,128)(2,1)S(1)}, bf16[128,256]{1,0:T(8,128)(2,1)}, u32[]{:S(2)}) copy-start(bf16[128,256]{1,0:T(8,128)(2,1)} %own_ref.1) | copy-start | bytes 196612
  52.0 34.5 %copy-start.5 = (bf16[128,256]{1,0:T(8,128)(2,1)S(1)}, bf16[128,256]{1,0:T(8,128)(2,1)}, u32[]{:S(2)}) copy-start(bf16[128,256]{1,0:T(8,128)(2,1)} %cot_ref.1) | copy-start | bytes 196612
  87.6 26.6 %all-to-all-start.2 = ((bf16[16,64,128]{2,1,0:T(8,128)(2,1)}), bf16[16,64,128]{2,1,0:T(8,128)(2,1)S(1)}, u32[]{:S(2)}, u32[]{:S(2)}) async-start(bf16[16,64,128]{2,1,0:T(8,128)(2,1)} %get-tuple-element.16), calls=%async_computation.2 | async-start | bytes 524288 | tf_op jit(solution)/shard_map/all_to_all | solution.py:191
  130.4 14.6 %all-to-all-start.5 = ((f32[8,32,256]{2,1,0:T(8,128)}), f32[8,32,256]{2,1,0:T(8,128)S(1)}, u32[]{:S(2)}, u32[]{:S(2)}) async-start(f32[8,32,256]{2,1,0:T(8,128)} %shard_map.132.after_ref), calls=%async_computation.5 | async-start | bytes 524288 | tf_op jit(solution)/shard_map/all_to_all | solution.py:199
  145.0 36.3 %all-to-all-start.4 = ((bf16[64,32,256]{2,1,0:T(8,128)(2,1)}), bf16[64,32,256]{2,1,0:T(8,128)(2,1)S(1)}, u32[]{:S(2)}, u32[]{:S(2)}) async-start(bf16[64,32,256]{2,1,0:T(8,128)(2,1)} %bitcast.3), calls=%async_computation.4 | async-start | bytes 2097152 | tf_op jit(solution)/shard_map/all_to_all | solution.py:204

commit v4 on v3

--- a/solution.py
+++ b/solution.py
@@ -132,12 +132,6 @@
     one = one_ref[...]
     for k in range(out_ref.shape[0]):
         out_ref[k] = one
-
-
-def sum_repeat_step(parts_ref, out_ref):
-    total = jnp.sum(parts_ref[...], axis=0)
-    for k in range(out_ref.shape[0]):
-        out_ref[k] = total
 
 
 def sum_step(parts_ref, out_ref):
@@ -190,19 +184,22 @@
 
     swapped = lax.all_to_all(swap, COL, 0, 0, tiled=True)
     heads = lax.all_gather(head, COL, axis=0, tiled=True)
-    grads = call(
+    grads_own = call(
         grad_step, [VMEM] * 2, sds((n_y, 2 * SHARE, width), F32),
         [pltpu.VMEM((rows, width), BF16)],
     )(heads, swapped)
-    grads = lax.all_to_all(grads, "y", 0, 0, tiled=True)
-    grads = call(sum_repeat_step, [VMEM], sds((n_x, 2 * SHARE, width), F32))(grads)
-    grads_x = lax.all_to_all(grads, "x", 0, 0, tiled=True)
+    grads = lax.psum_scatter(
+        grads_own.reshape(-1, width), "y", scatter_dimension=0, tiled=True
+    )
+    grads = call(repeat_step, [VMEM], sds((n_x, 2 * SHARE, width), F32))(grads)
+    grads = lax.psum_scatter(
+        grads.reshape(-1, width), "x", scatter_dimension=0, tiled=True
+    )
     source_part = call(
         backward_tiles, slots + [VMEM] * 3 + [pl.BlockSpec(memory_space=pl.ANY)], sds((CB * TILE, width), BF16),
         [pltpu.VMEM((rows, width), BF16)] * 2 + [pltpu.VMEM((CB * TILE, width), F32)],
-    )(tile_count, tile_rows, tile_cols, tile_vals, heads, swapped, w_neigh, grads)
+    )(tile_count, tile_rows, tile_cols, tile_vals, heads, swapped, w_neigh, grads_own)
     source_parts = lax.all_to_all(source_part, ROW, 0, 0, tiled=True)
-    grads = jnp.sum(grads_x, axis=0)
     all_grads = lax.all_gather(grads, COL, axis=0, tiled=False)
     d_source = call(sum_step, [VMEM], sds(source_feats.shape, BF16))(
         source_parts.reshape(n_row, -1, width)

time: 183 us -> 255 us (1.39)
  the two profiles are of different devices: /device:TPU:4 before, /device:TPU:1 now
where the time goes in v4:
time: 255 us
  waiting for transfers between devices  108 us (42%)
  blocking collectives  82.3 us (32%)
  starting transfers between devices  39.1 us (15%)
  between operations  14.8 us (6%)
  Pallas kernels  7.22 us (3%)
  local copies, waits for them, and re-layouts  3.46 us (1%)
    reduce_scatter x1, waiting for transfers between devices, on_device(): lax.psum_scatter(grads_own.reshape(-1, width), 'y', scatter_dimension=0,...  42.9 us
    reduce_scatter x1, waiting for transfers between devices, on_device(): lax.psum_scatter(grads.reshape(-1, width), 'x', scatter_dimension=0, tile...  40.4 us
    all_to_all x1, blocking collectives, on_device(): parts = lax.all_to_all(pair, 'z', 0, 0, tiled=True)  32 us
    all_gather x1, blocking collectives, on_device(): all_grads = lax.all_gather(grads, COL, axis=0, tiled=False)  27.1 us
    all_gather x1, blocking collectives, on_device(): heads = lax.all_gather(head, COL, axis=0, tiled=True)  23.1 us
    all_to_all x1, waiting for transfers between devices, on_device(): lax.all_to_all(call(repeat_step, [VMEM], sds((n_row, own_source, width),...  22.1 us
    all_to_all x1, starting transfers between devices, on_device(): lax.all_to_all(call(repeat_step, [VMEM], sds((n_row, own_source, width),...  14 us
    ppermute x1, starting transfers between devices, on_device(): got = lax.ppermute(send, 'core', [(0, 1), (1, 0)])  11.8 us
  transfers between devices with their start and end apart: 6, of which 4 were waited for; matrix products, arithmetic and copies ran while one was open for 0% of the time, Pallas kernels for 0%

profile of v4, /device:TPU:1, one launch (start us, length us, event | category | flops | bytes accessed | tf_op | source)
XLA Modules:
  0.0 254.7 jit_solution(4038618679657196389)
XLA Ops:
  7.2 0.0 copy-start
  7.2 0.0 copy-start.7
  7.2 0.8 copy-done.7
  8.0 0.0 copy-start.8
  8.0 0.0 copy-start.9
  8.0 0.1 shard_map.128
  8.1 0.0 copy-start.1
  8.1 1.0 copy-done.1
  9.1 14.0 %all-to-all-start = ((bf16[64,32,256]{2,1,0:T(8,128)(2,1)}), bf16[64,32,256]{2,1,0:T(8,128)(2,1)S(1)}, u32[]{:S(2)}, u32[]{:S(2)}) async-start(bf16[64,32,256]{2,1,0:T(8,128)(2,1)} %copy-done.1), calls=%async_computation | async-start | bytes 2097152 | tf_op jit(solution)/shard_map/all_to_all | solution.py:166
  23.8 22.1 %all-to-all-done = bf16[64,32,256]{2,1,0:T(8,128)(2,1)S(1)} async-done(((bf16[64,32,256]{2,1,0:T(8,128)(2,1)}), bf16[64,32,256]{2,1,0:T(8,128)(2,1)S(1)}, u32[]{:S(2)}, u32[]{:S(2)}) %all-to-all-start) | async-done | bytes 1048608 | tf_op jit(solution)/shard_map/all_to_all | solution.py:166
  46.0 0.0 copy-done
  46.0 0.0 copy-done.8
  46.0 0.0 copy-done.9
  46.0 1.0 shard_map.129
  47.0 11.8 %collective-permute-start = (bf16[1024,256]{1,0:T(8,128)(2,1)S(1)}, bf16[1024,256]{1,0:T(8,128)(2,1)S(1)}, u32[]{:S(2)}, u32[]{:S(2)}) collective-permute-start(bf16[1024,256]{1,0:T(8,128)(2,1)S(1)} %get-tuple-element.12), channel_id=1, source_target_pairs={{0,1},{1,0},{2,3},{3,2},{4,5},{5,4},{6,7},{7,6},{8,9},{9,8},{10,11... | collective-permute-start | bytes 1572872 | tf_op jit(solution)/shard_map/ppermute | solution.py:176
  58.8 1.5 collective-permute-done
  60.4 0.0 copy-start.2
  60.4 0.0 copy-start.3
  60.4 0.0 copy-start.4
  60.4 0.0 copy-start.5
  60.4 0.1 add_convert_fusion
  60.5 32.0 %all_to_all.28.parts_ref = bf16[8,128,256]{2,1,0:T(8,128)(2,1)S(1)} all-to-all(bf16[8,128,256]{2,1,0:T(8,128)(2,1)S(1)} %bitcast.15), channel_id=1, replica_groups=mesh['x'=8,'y'=8,'z'=8,'core'=2] {'z'}, dimensions={0} | all-to-all | bytes 1048576 | tf_op jit(solution)/shard_map/all_to_all | solution.py:178
  92.5 0.0 copy-done.2
  92.5 0.0 copy-done.3
  92.5 0.0 copy-done.4
  92.5 0.0 copy-done.5
  92.5 1.1 shard_map.130
  93.6 5.1 %all-to-all-start.2 = ((bf16[16,64,128]{2,1,0:T(8,128)(2,1)}), bf16[16,64,128]{2,1,0:T(8,128)(2,1)S(1)}, u32[]{:S(2)}, u32[]{:S(2)}) async-start(bf16[16,64,128]{2,1,0:T(8,128)(2,1)} %get-tuple-element.16), calls=%async_computation.2 | async-start | bytes 524288 | tf_op jit(solution)/shard_map/all_to_all | solution.py:185
  98.8 23.1 %all_gather.9.head_ref = bf16[1792,256]{1,0:T(8,128)(2,1)S(1)} all-gather(bf16[112,256]{1,0:T(8,128)(2,1)S(1)} %get-tuple-element.15), channel_id=1, replica_groups=mesh['x'=8,'y'=8,'z'=8,'core'=2] {'z','core'}, dimensions={0}, use_global_device_ids=true | all-gather | bytes 974848 | tf_op jit(solution)/shard_map/all_gather | solution.py:186
  121.9 0.0 all-to-all-done.2.swap_ref
  121.9 1.0 shard_map.131.after_ref
  122.9 2.5 shard_map.132
  125.4 8.0 %all-to-all-start.3 = ((bf16[64,32,256]{2,1,0:T(8,128)(2,1)}), bf16[64,32,256]{2,1,0:T(8,128)(2,1)S(1)}, u32[]{:S(2)}, u32[]{:S(2)}) async-start(bf16[64,32,256]{2,1,0:T(8,128)(2,1)} %bitcast.3), calls=%async_computation.3 | async-start | bytes 2097152 | tf_op jit(solution)/shard_map/all_to_all | solution.py:202
  133.4 0.0 reduce-scatter.3.cloned.1.call-start
  133.4 0.7 reduce-scatter.3.cloned.1.call-update
  134.1 0.0 reduce-scatter.5.cloned.1.call-start
  134.2 42.9 %reduce-scatter.3.cloned.1.call-done.one_ref = f32[32,256]{1,0:T(8,128)} async-done(((f32[256,256]{1,0:T(8,128)}), f32[32,256]{1,0:T(8,128)}) %reduce-scatter.3.cloned.1.call-update) | async-done | bytes 32784 | tf_op jit(solution)/shard_map/reduce_scatter | solution.py:191
  177.1 0.0 copy-start.6
  177.1 0.8 copy-done.6
  177.9 0.7 shard_map.134
  178.6 0.0 reduce-scatter.5.cloned.1.call-update
  178.6 40.4 %reduce-scatter.5.cloned.1.call-done = f32[32,256]{1,0:T(8,128)} async-done(((f32[256,256]{1,0:T(8,128)}), f32[32,256]{1,0:T(8,128)}) %reduce-scatter.5.cloned.1.call-update) | async-done | bytes 32784 | tf_op jit(solution)/shard_map/reduce_scatter | solution.py:195
  219.1 27.1 %all-gather = f32[512,256]{1,0:T(8,128)S(1)} all-gather(f32[32,256]{1,0:T(8,128)} %reduce-scatter.5.cloned.1.call-done), channel_id=2, replica_groups=mesh['x'=8,'y'=8,'z'=8,'core'=2] {'z','core'}, dimensions={0}, use_global_device_ids=true | all-gather | bytes 557056 | tf_op jit(solution)/shard_map/all_gather | solution.py:203
  246.2 0.8 fusion
  247.0 0.0 all-to-all-done.3.parts_ref
  247.0 0.8 shard_map.133
  (1 shorter events, 0.0 us)
Async XLA Ops:
  7.2 38.8 %copy-start = (bf16[1,1,48,128,128]{4,3,2,1,0:T(8,128)(2,1)S(1)}, bf16[1,1,48,128,128]{4,3,2,1,0:T(8,128)(2,1)}, u32[]{:S(2)}) copy-start(bf16[1,1,48,128,128]{4,3,2,1,0:T(8,128)(2,1)} %vals_ref.3) | copy-start | bytes 4718596
  7.2 0.8 copy-start.7
  8.0 38.0 %copy-start.8 = (s32[1,1,48]{2,1,0:T(1,128)S(1)}, s32[1,1,48]{2,1,0:T(1,128)}, u32[]{:S(2)}) copy-start(s32[1,1,48]{2,1,0:T(1,128)} %rows_ref.3) | copy-start | bytes 580
  8.0 38.0 %copy-start.9 = (s32[1,1,48]{2,1,0:T(1,128)S(1)}, s32[1,1,48]{2,1,0:T(1,128)}, u32[]{:S(2)}) copy-start(s32[1,1,48]{2,1,0:T(1,128)} %cols_ref.3) | copy-start | bytes 580
  8.1 1.0 copy-start.1
  9.1 36.8 %all-to-all-start = ((bf16[64,32,256]{2,1,0:T(8,128)(2,1)}), bf16[64,32,256]{2,1,0:T(8,128)(2,1)S(1)}, u32[]{:S(2)}, u32[]{:S(2)}) async-start(bf16[64,32,256]{2,1,0:T(8,128)(2,1)} %copy-done.1), calls=%async_computation | async-start | bytes 2097152 | tf_op jit(solution)/shard_map/all_to_all | solution.py:166
  47.0 13.3 %collective-permute-start = (bf16[1024,256]{1,0:T(8,128)(2,1)S(1)}, bf16[1024,256]{1,0:T(8,128)(2,1)S(1)}, u32[]{:S(2)}, u32[]{:S(2)}) collective-permute-start(bf16[1024,256]{1,0:T(8,128)(2,1)S(1)} %get-tuple-element.12), channel_id=1, source_target_pairs={{0,1},{1,0},{2,3},{3,2},{4,5},{5,4},{6,7},{7,6},{8,9},{9,8},{10,11... | collective-permute-start | bytes 1572872 | tf_op jit(solution)/shard_map/ppermute | solution.py:176
  60.4 32.2 %copy-start.2 = (bf16[256,256]{1,0:T(8,128)(2,1)S(1)}, bf16[256,256]{1,0:T(8,128)(2,1)}, u32[]{:S(2)}) copy-start(bf16[256,256]{1,0:T(8,128)(2,1)} %w_neigh_ref.3) | copy-start | bytes 393220
  60.4 32.2 %copy-start.3 = (bf16[256,256]{1,0:T(8,128)(2,1)S(1)}, bf16[256,256]{1,0:T(8,128)(2,1)}, u32[]{:S(2)}) copy-start(bf16[256,256]{1,0:T(8,128)(2,1)} %w_self_ref.1) | copy-start | bytes 393220
  60.4 32.2 %copy-start.4 = (bf16[128,256]{1,0:T(8,128)(2,1)S(1)}, bf16[128,256]{1,0:T(8,128)(2,1)}, u32[]{:S(2)}) copy-start(bf16[128,256]{1,0:T(8,128)(2,1)} %own_ref.1) | copy-start | bytes 196612
  60.4 32.2 %copy-start.5 = (bf16[128,256]{1,0:T(8,128)(2,1)S(1)}, bf16[128,256]{1,0:T(8,128)(2,1)}, u32[]{:S(2)}) copy-start(bf16[128,256]{1,0:T(8,128)(2,1)} %cot_ref.1) | copy-start | bytes 196612
  93.6 28.3 %all-to-all-start.2 = ((bf16[16,64,128]{2,1,0:T(8,128)(2,1)}), bf16[16,64,128]{2,1,0:T(8,128)(2,1)S(1)}, u32[]{:S(2)}, u32[]{:S(2)}) async-start(bf16[16,64,128]{2,1,0:T(8,128)(2,1)} %get-tuple-element.16), calls=%async_computation.2 | async-start | bytes 524288 | tf_op jit(solution)/shard_map/all_to_all | solution.py:185
  125.4 121.7 %all-to-all-start.3 = ((bf16[64,32,256]{2,1,0:T(8,128)(2,1)}), bf16[64,32,256]{2,1,0:T(8,128)(2,1)S(1)}, u32[]{:S(2)}, u32[]{:S(2)}) async-start(bf16[64,32,256]{2,1,0:T(8,128)(2,1)} %bitcast.3), calls=%async_computation.3 | async-start | bytes 2097152 | tf_op jit(solution)/shard_map/all_to_all | solution.py:202
  133.4 43.7 %reduce-scatter.3.cloned.1.call-start = ((), (), s32[]{:S(2)}) async-start(), calls=%async_computation.6 | async-start | bytes 294912 | tf_op jit(solution)/shard_map/reduce_scatter | solution.py:191
  134.1 84.9 %reduce-scatter.5.cloned.1.call-start = ((), (), s32[]{:S(2)}) async-start(), calls=%async_computation.7 | async-start | bytes 294912 | tf_op jit(solution)/shard_map/reduce_scatter | solution.py:195
  177.1 0.8 copy-start.6
Sparse Core Ops, SparseCore 0:
  138.2 38.9 reduce-scatter.2
  181.4 37.5 reduce-scatter.4

commit v5 on v2

--- a/solution.py
+++ b/solution.py
@@ -17,6 +17,7 @@
 BF16 = jnp.bfloat16
 VMEM = pl.BlockSpec(memory_space=pltpu.VMEM)
 SMEM = pl.BlockSpec(memory_space=pltpu.SMEM)
+ANY = pl.BlockSpec(memory_space=pl.ANY)
 PARAMS = pltpu.CompilerParams(vmem_limit_bytes=32 * 1024 * 1024)
 
 
@@ -85,7 +86,11 @@
         return carry
 
     lax.fori_loop(0, live_groups(count_ref), group, 0)
-    out_ref[...] = total[...].astype(BF16)
+    n = out_ref.shape[0]
+    share = total.shape[0] // n
+    for k in range(n):
+        out_ref[k, :share, :] = total[k * share : (k + 1) * share, :].astype(BF16)
+        out_ref[k, share:, :] = jnp.zeros((out_ref.shape[1] - share, total.shape[1]), BF16)
 
 
 def dense_step(
@@ -124,21 +129,68 @@
             swap_ref[k, : 2 * SHARE, :], d_pre[k * TILE : (k + 1) * TILE, :],
             preferred_element_type=F32,
         )
-    out_ref[...] = total
+    for k in range(out_ref.shape[0]):
+        out_ref[k] = total
+
+
+def repeat_step(one_ref, out_ref, sems):
+    copies = [
+        pltpu.make_async_copy(one_ref, out_ref.at[k], sems.at[k]) for k in range(out_ref.shape[0])
+    ]
+    for copy in copies:
+        copy.start()
+    for copy in copies:
+        copy.wait()
+
+
+def place_step(parts_ref, blocks_ref, out_ref, total, sems):
+    del blocks_ref
+    n = out_ref.shape[0]
+    rows = total.shape[0]
+    first = out_ref.shape[1] - rows
+    total[...] = jnp.sum(parts_ref[...], axis=0).astype(BF16)
+    copies = [
+        pltpu.make_async_copy(total, out_ref.at[k, pl.ds(first, rows)], sems.at[k])
+        for k in range(n)
+    ]
+    for copy in copies:
+        copy.start()
+    for copy in copies:
+        copy.wait()
+
+
+def stage_sum(parts_ref, source_ref):
+    rows = source_ref.shape[0]
+    source_ref[...] = jnp.sum(parts_ref[:, :rows, :].astype(F32), axis=0).astype(BF16)
+
+
+def split_grads(parts_ref, after_ref, neigh_ref, self_ref):
+    del after_ref
+    for k in range(parts_ref.shape[0]):
+        rows = slice(k * SHARE, (k + 1) * SHARE)
+        neigh_ref[rows, :] = parts_ref[k, :SHARE, :]
+        self_ref[rows, :] = parts_ref[k, SHARE:, :]
+
+
+def stage_grads(parts_ref, after_ref, grads_ref):
+    del after_ref
+    rows = grads_ref.shape[0]
+    grads_ref[...] = jnp.sum(parts_ref[:, parts_ref.shape[1] - rows :, :].astype(F32), axis=0)
 
 
 def sum_step(parts_ref, out_ref):
     out_ref[...] = jnp.sum(parts_ref[...].astype(F32), axis=0).astype(BF16)
 
 
-def call(kernel, ins, outs, scratch=()):
+def call(kernel, ins, outs, scratch=(), out_spec=VMEM, aliases=None):
     single = not isinstance(outs, list)
     return pl.pallas_call(
         kernel,
         out_shape=outs,
         in_specs=ins,
-        out_specs=VMEM if single else [VMEM] * len(outs),
+        out_specs=out_spec if single else [out_spec] * len(outs),
         scratch_shapes=scratch,
+        input_output_aliases=aliases or {},
         compiler_params=PARAMS,
     )
 
@@ -157,7 +209,11 @@
     rows = RB * TILE
 
     block_source = lax.all_to_all(
-        jnp.broadcast_to(source_feats[None], (n_row, own_source, width)), ROW, 0, 0, tiled=True
+        call(
+            repeat_step, [ANY], sds((n_row, own_source, width), BF16),
+            [pltpu.SemaphoreType.DMA((n_row,))], ANY,
+        )(source_feats),
+        ROW, 0, 0, tiled=True,
     ).reshape(rows, width)
     core = lax.axis_index("core").astype(jnp.int32).reshape(1, 1)
     mine, send = call(
@@ -177,27 +233,31 @@
     swapped = lax.all_to_all(swap, COL, 0, 0, tiled=True)
     heads = lax.all_gather(head, COL, axis=0, tiled=True)
     grads = call(
-        grad_step, [VMEM] * 2, sds((2 * SHARE, width), F32),
+        grad_step, [VMEM] * 2, sds((n_y, 2 * SHARE, width), F32),
         [pltpu.VMEM((rows, width), BF16)],
     )(heads, swapped)
-    grads_y = lax.all_to_all(
-        jnp.broadcast_to(grads[None], (n_y,) + grads.shape), "y", 0, 0, tiled=True
-    )
-    source_part = call(
-        backward_tiles, slots + [VMEM] * 3, sds((CB * TILE, width), BF16),
+    grads_y = lax.all_to_all(grads, "y", 0, 0, tiled=True)
+    blocks = call(
+        backward_tiles, slots + [VMEM] * 3,
+        sds((n_x, rows // n_x + 2 * SHARE, width), BF16),
         [pltpu.VMEM((rows, width), BF16)] * 2 + [pltpu.VMEM((CB * TILE, width), F32)],
     )(tile_count, tile_rows, tile_cols, tile_vals, heads, swapped, w_neigh)
-    source_parts = lax.all_to_all(source_part, ROW, 0, 0, tiled=True)
-    grads = jnp.sum(grads_y, axis=0)
-    grads_x = lax.all_gather(grads, ("x", "core"), axis=0, tiled=False)
-    grads_x = grads_x.reshape((n_x, 2) + grads.shape)
-    grads = jnp.sum(lax.dynamic_index_in_dim(grads_x, core[0, 0], 1, keepdims=False), axis=0)
+    blocks = call(
+        place_step, [VMEM, ANY], sds(blocks.shape, BF16),
+        [pltpu.VMEM((2 * SHARE, width), BF16), pltpu.SemaphoreType.DMA((n_x,))], ANY, {1: 0},
+    )(grads_y, blocks)
+    blocks = lax.all_to_all(blocks, "x", 0, 0, tiled=True)
+    source_y = call(stage_sum, [VMEM], sds((rows // n_x, width), BF16))(blocks)
+    grads = call(stage_grads, [VMEM, ANY], sds((2 * SHARE, width), F32))(blocks, source_y)
+    source_parts = lax.all_to_all(source_y, "y", 0, 0, tiled=True)
     all_grads = lax.all_gather(grads, COL, axis=0, tiled=False)
     d_source = call(sum_step, [VMEM], sds(source_feats.shape, BF16))(
-        source_parts.reshape(n_row, -1, width)
-    )
-    all_grads = all_grads.reshape(n_col, 2, SHARE, width).swapaxes(0, 1).reshape(2, width, width)
-    return (layer_out, d_target, d_source, all_grads[0], all_grads[1])
+        source_parts.reshape(n_y, -1, width)
+    )
+    grad_neigh, grad_self = call(
+        split_grads, [VMEM, ANY], [sds((width, width), F32)] * 2
+    )(all_grads, d_source)
+    return (layer_out, d_target, d_source, grad_neigh, grad_self)
 
 
 def solution(mesh):

time: 194 us -> 194 us (level)
  blocking collectives: 110 us -> 107 us
    all_gather x1 -> x0, blocking collectives: 37.8 us -> none  [on_device(): grads_x = lax.all_gather(grads, ('x', 'core'), axis=0, tiled=False)]
    all_to_all x0 -> x1, blocking collectives: none -> 33.8 us  [on_device(): blocks = lax.all_to_all(blocks, 'x', 0, 0, tiled=True)]
    unnamed x14 -> x22, local copies, waits for them, and re-layouts: 0.03 us -> 3.85 us
    broadcast_in_dim x2 -> x0, local copies, waits for them, and re-layouts: 2.67 us -> none  [the longest x1 1.93 us: on_device(): jnp.broadcast_to(source_feats[None], (n_row, own_source, width))]
    pallas_call x2 -> x7, Pallas kernels: 4.36 us -> 6.41 us  [the longest x1 2.02 us: on_device(): call(repeat_step, [ANY], sds((n_row, own_source, width), BF16), [pltpu.Se...]
  transfers between devices with their start and end apart: 5 -> 5, of which waited for: 3 -> 3; matrix products, arithmetic and copies ran while one was open for 0% -> 0% of each run, Pallas kernels for 2% -> 1%
where the time goes in v5:
time: 194 us; the launch traced here: 193 us
  blocking collectives  107 us (55%)
  starting transfers between devices  38.3 us (20%)
  waiting for transfers between devices  33 us (17%)
  Pallas kernels  9.19 us (5%)
  local copies, waits for them, and re-layouts  3.85 us (2%)
    all_to_all x1, blocking collectives, on_device(): blocks = lax.all_to_all(blocks, 'x', 0, 0, tiled=True)  33.8 us
    all_to_all x1, blocking collectives, on_device(): parts = lax.all_to_all(pair, 'z', 0, 0, tiled=True)  32.3 us
    all_gather x1, blocking collectives, on_device(): heads = lax.all_gather(head, COL, axis=0, tiled=True)  23.1 us
    all_to_all x1, waiting for transfers between devices, on_device(): lax.all_to_all(call(repeat_step, [ANY], sds((n_row, own_source, width), B...  22.1 us
    all_gather x1, blocking collectives, on_device(): all_grads = lax.all_gather(grads, COL, axis=0, tiled=False)  18 us
    all_to_all x1, starting transfers between devices, on_device(): lax.all_to_all(call(repeat_step, [ANY], sds((n_row, own_source, width), B...  14.2 us
    ppermute x1, starting transfers between devices, on_device(): got = lax.ppermute(send, 'core', [(0, 1), (1, 0)])  10.7 us
    all_to_all x1, waiting for transfers between devices, on_device(): grads_y = lax.all_to_all(grads, 'y', 0, 0, tiled=True)  9.36 us
  transfers between devices with their start and end apart: 5, of which 3 were waited for; matrix products, arithmetic and copies ran while one was open for 0% of the time, Pallas kernels for 1%

profile of v5, /device:TPU:1, one launch (start us, length us, event | category | flops | bytes accessed | tf_op | source)
XLA Modules:
  0.0 193.1 jit_solution(3080570735558555853)
XLA Ops:
  0.6 0.0 copy-start.8
  0.6 0.7 copy-done.8
  1.3 2.0 %shard_map.128 = bf16[64,32,256]{2,1,0:T(8,128)(2,1)S(1)} custom-call(bf16[32,256]{1,0:T(8,128)(2,1)S(1)} %copy-done.8), custom_call_target="tpu_custom_call" | custom-call | tf_op jit(solution)/shard_map/pallas_call | solution.py:212
  3.4 0.0 copy-start.2
  3.4 1.0 copy-done.2
  4.4 0.0 copy-start
  4.4 0.0 copy-start.9
  4.4 0.0 copy-start.10
  4.4 14.2 %all-to-all-start = ((bf16[64,32,256]{2,1,0:T(8,128)(2,1)}), bf16[64,32,256]{2,1,0:T(8,128)(2,1)S(1)}, u32[]{:S(2)}, u32[]{:S(2)}) async-start(bf16[64,32,256]{2,1,0:T(8,128)(2,1)} %copy-done.2), calls=%async_computation | async-start | bytes 2097152 | tf_op jit(solution)/shard_map/all_to_all | solution.py:211
  19.2 22.1 %all-to-all-done = bf16[64,32,256]{2,1,0:T(8,128)(2,1)S(1)} async-done(((bf16[64,32,256]{2,1,0:T(8,128)(2,1)}), bf16[64,32,256]{2,1,0:T(8,128)(2,1)S(1)}, u32[]{:S(2)}, u32[]{:S(2)}) %all-to-all-start) | async-done | bytes 1048608 | tf_op jit(solution)/shard_map/all_to_all | solution.py:211
  41.4 0.0 copy-done
  41.4 0.0 copy-done.9
  41.4 0.0 copy-done.10
  41.4 1.0 shard_map.129
  42.4 10.7 %collective-permute-start = (bf16[1024,256]{1,0:T(8,128)(2,1)S(1)}, bf16[1024,256]{1,0:T(8,128)(2,1)S(1)}, u32[]{:S(2)}, u32[]{:S(2)}) collective-permute-start(bf16[1024,256]{1,0:T(8,128)(2,1)S(1)} %get-tuple-element.14), channel_id=1, source_target_pairs={{0,1},{1,0},{2,3},{3,2},{4,5},{5,4},{6,7},{7,6},{8,9},{9,8},{10,11... | collective-permute-start | bytes 1572872 | tf_op jit(solution)/shard_map/ppermute | solution.py:224
  53.1 1.5 collective-permute-done
  54.6 0.0 copy-start.3
  54.6 0.0 copy-start.4
  54.6 0.0 copy-start.5
  54.6 0.0 copy-start.6
  54.6 0.1 add_convert_fusion
  54.7 32.3 %all_to_all.38.parts_ref = bf16[8,128,256]{2,1,0:T(8,128)(2,1)S(1)} all-to-all(bf16[8,128,256]{2,1,0:T(8,128)(2,1)S(1)} %bitcast.7), channel_id=1, replica_groups=mesh['x'=8,'y'=8,'z'=8,'core'=2] {'z'}, dimensions={0} | all-to-all | bytes 1048576 | tf_op jit(solution)/shard_map/all_to_all | solution.py:226
  87.0 0.0 copy-done.3
  87.0 0.0 copy-done.4
  87.0 0.0 copy-done.5
  87.0 0.0 copy-done.6
  87.0 1.1 shard_map.130
  88.1 5.1 %all-to-all-start.2 = ((bf16[16,64,128]{2,1,0:T(8,128)(2,1)}), bf16[16,64,128]{2,1,0:T(8,128)(2,1)S(1)}, u32[]{:S(2)}, u32[]{:S(2)}) async-start(bf16[16,64,128]{2,1,0:T(8,128)(2,1)} %get-tuple-element.18), calls=%async_computation.2 | async-start | bytes 524288 | tf_op jit(solution)/shard_map/all_to_all | solution.py:233
  93.2 23.1 %all_gather.9.head_ref = bf16[1792,256]{1,0:T(8,128)(2,1)S(1)} all-gather(bf16[112,256]{1,0:T(8,128)(2,1)S(1)} %get-tuple-element.17), channel_id=1, replica_groups=mesh['x'=8,'y'=8,'z'=8,'core'=2] {'z','core'}, dimensions={0}, use_global_device_ids=true | all-gather | bytes 974848 | tf_op jit(solution)/shard_map/all_gather | solution.py:234
  116.4 0.0 all-to-all-done.2.swap_ref
  116.4 1.0 shard_map.131
  117.4 5.0 %all-to-all-start.3 = ((f32[8,32,256]{2,1,0:T(8,128)}), f32[8,32,256]{2,1,0:T(8,128)S(1)}, u32[]{:S(2)}, u32[]{:S(2)}) async-start(f32[8,32,256]{2,1,0:T(8,128)} %shard_map.131), calls=%async_computation.3 | async-start | bytes 524288 | tf_op jit(solution)/shard_map/all_to_all | solution.py:239
  122.4 0.0 copy-start.1
  122.4 1.4 copy-done.1
  123.8 1.5 shard_map.132.blocks_ref
  125.3 9.4 %all-to-all-done.3.parts_ref = f32[8,32,256]{2,1,0:T(8,128)S(1)} async-done(((f32[8,32,256]{2,1,0:T(8,128)}), f32[8,32,256]{2,1,0:T(8,128)S(1)}, u32[]{:S(2)}, u32[]{:S(2)}) %all-to-all-start.3) | async-done | bytes 262176 | tf_op jit(solution)/shard_map/all_to_all | solution.py:239
  134.6 0.3 shard_map.133
  134.9 33.8 %all_to_all.39.parts_ref = bf16[8,288,256]{2,1,0:T(8,128)(2,1)S(1)} all-to-all(bf16[8,288,256]{2,1,0:T(8,128)(2,1)S(1)} %shard_map.133), channel_id=1, replica_groups=mesh['x'=8,'y'=8,'z'=8,'core'=2] {'x'}, dimensions={0} | all-to-all | bytes 2359296 | tf_op jit(solution)/shard_map/all_to_all | solution.py:249
  168.7 0.8 shard_map.134.after_ref
  169.5 3.4 %all-to-all-start.5 = ((bf16[8,32,256]{2,1,0:T(8,128)(2,1)}), bf16[8,32,256]{2,1,0:T(8,128)(2,1)S(1)}, u32[]{:S(2)}, u32[]{:S(2)}) async-start(bf16[8,32,256]{2,1,0:T(8,128)(2,1)} %bitcast.3), calls=%async_computation.5 | async-start | bytes 262144 | tf_op jit(solution)/shard_map/all_to_all | solution.py:252
  172.9 18.0 %all-gather = f32[512,256]{1,0:T(8,128)S(1)} all-gather(f32[32,256]{1,0:T(8,128)S(1)} %shard_map.136), channel_id=2, replica_groups=mesh['x'=8,'y'=8,'z'=8,'core'=2] {'z','core'}, dimensions={0}, use_global_device_ids=true | all-gather | bytes 557056 | tf_op jit(solution)/shard_map/all_gather | solution.py:253
  190.9 0.0 all-to-all-done.5.parts_ref
  190.9 0.6 shard_map.135.after_ref
  191.5 0.0 copy-start.7
  191.5 0.7 copy-done.7
  192.3 0.8 shard_map.137
  (1 shorter events, 0.0 us)
Async XLA Ops:
  0.6 0.7 copy-start.8
  3.4 1.0 copy-start.2
  4.4 37.0 %copy-start = (bf16[1,1,48,128,128]{4,3,2,1,0:T(8,128)(2,1)S(1)}, bf16[1,1,48,128,128]{4,3,2,1,0:T(8,128)(2,1)}, u32[]{:S(2)}) copy-start(bf16[1,1,48,128,128]{4,3,2,1,0:T(8,128)(2,1)} %vals_ref.3) | copy-start | bytes 4718596
  4.4 37.0 %copy-start.9 = (s32[1,1,48]{2,1,0:T(1,128)S(1)}, s32[1,1,48]{2,1,0:T(1,128)}, u32[]{:S(2)}) copy-start(s32[1,1,48]{2,1,0:T(1,128)} %rows_ref.3) | copy-start | bytes 580
  4.4 37.0 %copy-start.10 = (s32[1,1,48]{2,1,0:T(1,128)S(1)}, s32[1,1,48]{2,1,0:T(1,128)}, u32[]{:S(2)}) copy-start(s32[1,1,48]{2,1,0:T(1,128)} %cols_ref.3) | copy-start | bytes 580
  4.4 37.0 %all-to-all-start = ((bf16[64,32,256]{2,1,0:T(8,128)(2,1)}), bf16[64,32,256]{2,1,0:T(8,128)(2,1)S(1)}, u32[]{:S(2)}, u32[]{:S(2)}) async-start(bf16[64,32,256]{2,1,0:T(8,128)(2,1)} %copy-done.2), calls=%async_computation | async-start | bytes 2097152 | tf_op jit(solution)/shard_map/all_to_all | solution.py:211
  42.4 12.2 %collective-permute-start = (bf16[1024,256]{1,0:T(8,128)(2,1)S(1)}, bf16[1024,256]{1,0:T(8,128)(2,1)S(1)}, u32[]{:S(2)}, u32[]{:S(2)}) collective-permute-start(bf16[1024,256]{1,0:T(8,128)(2,1)S(1)} %get-tuple-element.14), channel_id=1, source_target_pairs={{0,1},{1,0},{2,3},{3,2},{4,5},{5,4},{6,7},{7,6},{8,9},{9,8},{10,11... | collective-permute-start | bytes 1572872 | tf_op jit(solution)/shard_map/ppermute | solution.py:224
  54.6 32.4 %copy-start.3 = (bf16[256,256]{1,0:T(8,128)(2,1)S(1)}, bf16[256,256]{1,0:T(8,128)(2,1)}, u32[]{:S(2)}) copy-start(bf16[256,256]{1,0:T(8,128)(2,1)} %w_neigh_ref.3) | copy-start | bytes 393220
  54.6 32.4 %copy-start.4 = (bf16[256,256]{1,0:T(8,128)(2,1)S(1)}, bf16[256,256]{1,0:T(8,128)(2,1)}, u32[]{:S(2)}) copy-start(bf16[256,256]{1,0:T(8,128)(2,1)} %w_self_ref.1) | copy-start | bytes 393220
  54.6 32.4 %copy-start.5 = (bf16[128,256]{1,0:T(8,128)(2,1)S(1)}, bf16[128,256]{1,0:T(8,128)(2,1)}, u32[]{:S(2)}) copy-start(bf16[128,256]{1,0:T(8,128)(2,1)} %own_ref.1) | copy-start | bytes 196612
  54.6 32.4 %copy-start.6 = (bf16[128,256]{1,0:T(8,128)(2,1)S(1)}, bf16[128,256]{1,0:T(8,128)(2,1)}, u32[]{:S(2)}) copy-start(bf16[128,256]{1,0:T(8,128)(2,1)} %cot_ref.1) | copy-start | bytes 196612
  88.1 28.3 %all-to-all-start.2 = ((bf16[16,64,128]{2,1,0:T(8,128)(2,1)}), bf16[16,64,128]{2,1,0:T(8,128)(2,1)S(1)}, u32[]{:S(2)}, u32[]{:S(2)}) async-start(bf16[16,64,128]{2,1,0:T(8,128)(2,1)} %get-tuple-element.18), calls=%async_computation.2 | async-start | bytes 524288 | tf_op jit(solution)/shard_map/all_to_all | solution.py:233
  117.4 17.3 %all-to-all-start.3 = ((f32[8,32,256]{2,1,0:T(8,128)}), f32[8,32,256]{2,1,0:T(8,128)S(1)}, u32[]{:S(2)}, u32[]{:S(2)}) async-start(f32[8,32,256]{2,1,0:T(8,128)} %shard_map.131), calls=%async_computation.3 | async-start | bytes 524288 | tf_op jit(solution)/shard_map/all_to_all | solution.py:239
  122.4 1.4 copy-start.1
  169.5 21.4 %all-to-all-start.5 = ((bf16[8,32,256]{2,1,0:T(8,128)(2,1)}), bf16[8,32,256]{2,1,0:T(8,128)(2,1)S(1)}, u32[]{:S(2)}, u32[]{:S(2)}) async-start(bf16[8,32,256]{2,1,0:T(8,128)(2,1)} %bitcast.3), calls=%async_computation.5 | async-start | bytes 262144 | tf_op jit(solution)/shard_map/all_to_all | solution.py:252
  191.5 0.7 copy-start.7

commit v6 on v3

--- a/solution.py
+++ b/solution.py
@@ -8,7 +8,8 @@
 RB = 16
 CB = 16
 TILE = 128
-GROUP = 4
+GROUP = 16
+REST = 8
 SHARE = 16
 TAIL = 16
 ROW = ("x", "y")
@@ -20,26 +21,41 @@
 PARAMS = pltpu.CompilerParams(vmem_limit_bytes=32 * 1024 * 1024)
 
 
-def live_groups(count_ref):
-    return (count_ref[0, 0] + (GROUP - 1)) // GROUP
-
-
-def forward_tiles(
-    core_ref, count_ref, rows_ref, cols_ref, vals_ref, src_ref, mine_ref, send_ref, total
-):
-    count = count_ref[0, 0]
-    total[...] = jnp.zeros_like(total)
+def live_tiles(count, add, product):
+    groups = count // GROUP
+    done = groups * GROUP
 
     def group(g, carry):
         for k in range(GROUP):
             s = g * GROUP + k
-            at = pl.ds(pl.multiple_of(rows_ref[0, 0, s] * TILE, TILE), TILE)
-            of = pl.ds(pl.multiple_of(cols_ref[0, 0, s] * TILE, TILE), TILE)
-            product = jnp.dot(vals_ref[0, 0, s], src_ref[of, :], preferred_element_type=F32)
-            total[at, :] += jnp.where(s < count, product, 0.0)
+            add(s, product(s))
         return carry
 
-    lax.fori_loop(0, live_groups(count_ref), group, 0)
+    def rest(g, carry):
+        for k in range(REST):
+            s = done + g * REST + k
+            add(s, jnp.where(s < count, product(s), 0.0))
+        return carry
+
+    lax.fori_loop(0, groups, group, 0)
+    lax.fori_loop(0, (count - done + (REST - 1)) // REST, rest, 0)
+
+
+def forward_tiles(
+    core_ref, count_ref, rows_ref, cols_ref, vals_ref, src_ref, mine_ref, send_ref, total
+):
+    count = count_ref[0, 0]
+    total[...] = jnp.zeros_like(total)
+
+    def product(s):
+        of = pl.ds(pl.multiple_of(cols_ref[0, 0, s] * TILE, TILE), TILE)
+        return jnp.dot(vals_ref[0, 0, s], src_ref[of, :], preferred_element_type=F32)
+
+    def add(s, value):
+        at = pl.ds(pl.multiple_of(rows_ref[0, 0, s] * TILE, TILE), TILE)
+        total[at, :] += value
+
+    live_tiles(count, add, product)
     core = core_ref[0, 0]
     share = mine_ref.shape[0] // (RB // 2)
     for k in range(RB // 2):
@@ -73,18 +89,17 @@
         d_pre[...], w_neigh_ref[...], (((1,), (1,)), ((), ())), preferred_element_type=F32
     ).astype(BF16)
 
-    def group(g, carry):
-        for k in range(GROUP):
-            s = g * GROUP + k
-            of = pl.ds(pl.multiple_of(rows_ref[0, 0, s] * TILE, TILE), TILE)
-            at = pl.ds(pl.multiple_of(cols_ref[0, 0, s] * TILE, TILE), TILE)
-            product = lax.dot_general(
-                vals_ref[0, 0, s], d_agg[of, :], (((0,), (0,)), ((), ())), preferred_element_type=F32
-            )
-            total[at, :] += jnp.where(s < count, product, 0.0)
-        return carry
-
-    lax.fori_loop(0, live_groups(count_ref), group, 0)
+    def product(s):
+        of = pl.ds(pl.multiple_of(rows_ref[0, 0, s] * TILE, TILE), TILE)
+        return lax.dot_general(
+            vals_ref[0, 0, s], d_agg[of, :], (((0,), (0,)), ((), ())), preferred_element_type=F32
+        )
+
+    def add(s, value):
+        at = pl.ds(pl.multiple_of(cols_ref[0, 0, s] * TILE, TILE), TILE)
+        total[at, :] += value
+
+    live_tiles(count, add, product)
     out_ref[...] = total[...].astype(BF16)
 
 
@@ -115,15 +130,16 @@
         swap_ref[k, 2 * SHARE + TAIL :, :] = d_pre[head:, half:]
 
 
-def grad_step(head_ref, swap_ref, out_ref, d_pre):
-    assemble(head_ref, swap_ref, d_pre)
+def grad_step(head_ref, swap_ref, out_ref):
     n = swap_ref.shape[0]
-    total = jnp.zeros((2 * SHARE, d_pre.shape[1]), F32)
+    head = head_ref.shape[0] // n
+    total = jnp.zeros(out_ref.shape[1:], F32)
     for k in range(n):
-        total += jnp.dot(
-            swap_ref[k, : 2 * SHARE, :], d_pre[k * TILE : (k + 1) * TILE, :],
-            preferred_element_type=F32,
+        tail = jnp.concatenate(
+            [swap_ref[k, 2 * SHARE : 2 * SHARE + TAIL, :], swap_ref[k, 2 * SHARE + TAIL :, :]], axis=1
         )
+        d_pre = jnp.concatenate([head_ref[k * head : (k + 1) * head, :], tail], axis=0)
+        total += jnp.dot(swap_ref[k, : 2 * SHARE, :], d_pre, preferred_element_type=F32)
     for k in range(out_ref.shape[0]):
         out_ref[k] = total
 
@@ -156,6 +172,18 @@
     )
 
 
+def repeat_rows(one, n):
+    step = max(n // 8, 1)
+    return pl.pallas_call(
+        repeat_step,
+        grid=(n // step,),
+        out_shape=jax.ShapeDtypeStruct((n,) + one.shape, one.dtype),
+        in_specs=[pl.BlockSpec(one.shape, lambda i: (0, 0))],
+        out_specs=pl.BlockSpec((step,) + one.shape, lambda i: (i, 0, 0)),
+        compiler_params=PARAMS,
+    )(one)
+
+
 def on_device(
     source_feats, target_feats, w_neigh, w_self, tile_count, tile_rows, tile_cols, tile_vals, cotangent
 ):
@@ -170,7 +198,7 @@
     rows = RB * TILE
 
     block_source = lax.all_to_all(
-        call(repeat_step, [VMEM], sds((n_row, own_source, width), BF16))(source_feats),
+        repeat_rows(source_feats, n_row),
         ROW, 0, 0, tiled=True,
     ).reshape(rows, width)
     core = lax.axis_index("core").astype(jnp.int32).reshape(1, 1)
@@ -192,7 +220,6 @@
     heads = lax.all_gather(head, COL, axis=0, tiled=True)
     grads = call(
         grad_step, [VMEM] * 2, sds((n_y, 2 * SHARE, width), F32),
-        [pltpu.VMEM((rows, width), BF16)],
     )(heads, swapped)
     grads = lax.all_to_all(grads, "y", 0, 0, tiled=True)
     grads = call(sum_repeat_step, [VMEM], sds((n_x, 2 * SHARE, width), F32))(grads)

time: 183 us -> 184 us (level)
  transfers between devices with their start and end apart: 5 -> 5, of which waited for: 4 -> 4; matrix products, arithmetic and copies ran while one was open for 0% -> 0% of each run, Pallas kernels for 2% -> 1%
where the time goes in v6:
time: 184 us; the launch traced here: 183 us
  blocking collectives  89.3 us (49%)
  waiting for transfers between devices  48 us (26%)
  starting transfers between devices  34.8 us (19%)
  Pallas kernels  6.71 us (4%)
  local copies, waits for them, and re-layouts  2.66 us (1%)
    all_to_all x1, blocking collectives, on_device(): parts = lax.all_to_all(pair, 'z', 0, 0, tiled=True)  35.1 us
    all_to_all x1, waiting for transfers between devices, on_device(): lax.all_to_all(repeat_rows(source_feats, n_row), ROW, 0, 0, tiled=True)  26 us
    all_gather x1, blocking collectives, on_device(): heads = lax.all_gather(head, COL, axis=0, tiled=True)  23.1 us
    all_to_all x1, starting transfers between devices, on_device(): lax.all_to_all(repeat_rows(source_feats, n_row), ROW, 0, 0, tiled=True)  17.3 us
    all_gather x1, blocking collectives, on_device(): all_grads = lax.all_gather(grads, COL, axis=0, tiled=False)  16 us
    all_to_all x1, blocking collectives, on_device(): grads = lax.all_to_all(grads, 'y', 0, 0, tiled=True)  15.1 us
    all_to_all x1, waiting for transfers between devices, on_device(): source_parts = lax.all_to_all(source_part, ROW, 0, 0, tiled=True)  13.4 us
    all_to_all x1, starting transfers between devices, on_device(): source_parts = lax.all_to_all(source_part, ROW, 0, 0, tiled=True)  7.23 us
  transfers between devices with their start and end apart: 5, of which 4 were waited for; matrix products, arithmetic and copies ran while one was open for 0% of the time, Pallas kernels for 1%

profile of v6, /device:TPU:4, one launch (start us, length us, event | category | flops | bytes accessed | tf_op | source)
XLA Modules:
  0.0 183.0 jit_solution(3708473723312812007)
XLA Ops:
  0.6 0.0 copy-start
  0.6 0.0 copy-start.6
  0.7 0.8 copy-done.6
  1.5 0.0 copy-start.7
  1.5 0.0 copy-start.8
  1.5 0.2 shard_map.128
  1.6 0.0 copy-start.1
  1.7 1.0 copy-done.1
  2.6 17.3 %all-to-all-start = ((bf16[64,32,256]{2,1,0:T(8,128)(2,1)}), bf16[64,32,256]{2,1,0:T(8,128)(2,1)S(1)}, u32[]{:S(2)}, u32[]{:S(2)}) async-start(bf16[64,32,256]{2,1,0:T(8,128)(2,1)} %copy-done.1), calls=%async_computation | async-start | bytes 2097152 | tf_op jit(solution)/shard_map/all_to_all | solution.py:200
  20.6 26.0 %all-to-all-done = bf16[64,32,256]{2,1,0:T(8,128)(2,1)S(1)} async-done(((bf16[64,32,256]{2,1,0:T(8,128)(2,1)}), bf16[64,32,256]{2,1,0:T(8,128)(2,1)S(1)}, u32[]{:S(2)}, u32[]{:S(2)}) %all-to-all-start) | async-done | bytes 1048608 | tf_op jit(solution)/shard_map/all_to_all | solution.py:200
  46.7 0.0 copy-done
  46.7 0.0 copy-done.7
  46.7 0.0 copy-done.8
  46.7 1.1 shard_map.129
  47.8 1.9 %collective-permute-start = (bf16[1024,256]{1,0:T(8,128)(2,1)S(1)}, bf16[1024,256]{1,0:T(8,128)(2,1)S(1)}, u32[]{:S(2)}, u32[]{:S(2)}) collective-permute-start(bf16[1024,256]{1,0:T(8,128)(2,1)S(1)} %get-tuple-element.12), channel_id=1, source_target_pairs={{0,1},{1,0},{2,3},{3,2},{4,5},{5,4},{6,7},{7,6},{8,9},{9,8},{10,11... | collective-permute-start | bytes 1572872 | tf_op jit(solution)/shard_map/ppermute | solution.py:210
  49.7 1.9 %collective-permute-done = bf16[1024,256]{1,0:T(8,128)(2,1)S(1)} collective-permute-done((bf16[1024,256]{1,0:T(8,128)(2,1)S(1)}, bf16[1024,256]{1,0:T(8,128)(2,1)S(1)}, u32[]{:S(2)}, u32[]{:S(2)}) %collective-permute-start) | collective-permute-done | bytes 524320 | tf_op jit(solution)/shard_map/ppermute | solution.py:210
  51.6 0.0 copy-start.2
  51.6 0.0 copy-start.3
  51.6 0.0 copy-start.4
  51.6 0.0 copy-start.5
  51.6 0.1 add_convert_fusion
  51.7 35.1 %all_to_all.38.parts_ref = bf16[8,128,256]{2,1,0:T(8,128)(2,1)S(1)} all-to-all(bf16[8,128,256]{2,1,0:T(8,128)(2,1)S(1)} %bitcast.11), channel_id=1, replica_groups=mesh['x'=8,'y'=8,'z'=8,'core'=2] {'z'}, dimensions={0} | all-to-all | bytes 1048576 | tf_op jit(solution)/shard_map/all_to_all | solution.py:212
  86.9 0.0 copy-done.2
  86.9 0.0 copy-done.3
  86.9 0.0 copy-done.4
  86.9 0.0 copy-done.5
  86.9 1.1 shard_map.130
  88.0 3.5 %all-to-all-start.2 = ((bf16[16,64,128]{2,1,0:T(8,128)(2,1)}), bf16[16,64,128]{2,1,0:T(8,128)(2,1)S(1)}, u32[]{:S(2)}, u32[]{:S(2)}) async-start(bf16[16,64,128]{2,1,0:T(8,128)(2,1)} %get-tuple-element.16), calls=%async_computation.2 | async-start | bytes 524288 | tf_op jit(solution)/shard_map/all_to_all | solution.py:219
  91.6 23.1 %all_gather.9.head_ref = bf16[1792,256]{1,0:T(8,128)(2,1)S(1)} all-gather(bf16[112,256]{1,0:T(8,128)(2,1)S(1)} %get-tuple-element.15), channel_id=1, replica_groups=mesh['x'=8,'y'=8,'z'=8,'core'=2] {'z','core'}, dimensions={0}, use_global_device_ids=true | all-gather | bytes 974848 | tf_op jit(solution)/shard_map/all_gather | solution.py:220
  114.6 0.0 all-to-all-done.2.swap_ref
  114.6 0.3 shard_map.131
  114.9 15.1 %all_to_all.39.parts_ref = f32[8,32,256]{2,1,0:T(8,128)S(1)} all-to-all(f32[8,32,256]{2,1,0:T(8,128)S(1)} %shard_map.131), channel_id=1, replica_groups=mesh['x'=8,'y'=8,'z'=8,'core'=2] {'y'}, dimensions={0} | all-to-all | bytes 524288 | tf_op jit(solution)/shard_map/all_to_all | solution.py:224
  130.0 0.7 shard_map.132.after_ref
  130.7 4.8 %all-to-all-start.5 = ((f32[8,32,256]{2,1,0:T(8,128)}), f32[8,32,256]{2,1,0:T(8,128)S(1)}, u32[]{:S(2)}, u32[]{:S(2)}) async-start(f32[8,32,256]{2,1,0:T(8,128)} %shard_map.132.after_ref), calls=%async_computation.5 | async-start | bytes 524288 | tf_op jit(solution)/shard_map/all_to_all | solution.py:226
  135.5 2.5 %shard_map.133 = bf16[2048,256]{1,0:T(8,128)(2,1)} custom-call(s32[1,1]{1,0:T(1,128)S(6)} %copy.14.count_ref, s32[1,1,48]{2,1,0:T(1,128)S(1)} %copy-done.7, s32[1,1,48]{2,1,0:T(1,128)S(1)} %copy-done.8, bf16[1,1,48,128,128]{4,3,2,1,0:T(8,128)(2,1)S(1)} %copy-done, bf16[1792,256]{1,0:T(8,128)(2,1)S(1)} %all_gather.9.head_ref, ...), custom_call_target="tpu_custom_call" | custom-call | tf_op jit(solution)/shard_map/pallas_call | solution.py:227
  138.1 6.7 %all-to-all-done.5 = f32[8,32,256]{2,1,0:T(8,128)S(1)} async-done(((f32[8,32,256]{2,1,0:T(8,128)}), f32[8,32,256]{2,1,0:T(8,128)S(1)}, u32[]{:S(2)}, u32[]{:S(2)}) %all-to-all-start.5) | async-done | bytes 262176 | tf_op jit(solution)/shard_map/all_to_all | solution.py:226
  144.8 7.2 %all-to-all-start.4 = ((bf16[64,32,256]{2,1,0:T(8,128)(2,1)}), bf16[64,32,256]{2,1,0:T(8,128)(2,1)S(1)}, u32[]{:S(2)}, u32[]{:S(2)}) async-start(bf16[64,32,256]{2,1,0:T(8,128)(2,1)} %bitcast.3), calls=%async_computation.4 | async-start | bytes 2097152 | tf_op jit(solution)/shard_map/all_to_all | solution.py:231
  152.0 16.0 %all-gather = f32[512,256]{1,0:T(8,128)S(1)} all-gather(f32[32,256]{1,0:T(8,128)S(1)} %reduce_sum.9), channel_id=2, replica_groups=mesh['x'=8,'y'=8,'z'=8,'core'=2] {'z','core'}, dimensions={0}, use_global_device_ids=true | all-gather | bytes 557056 | tf_op jit(solution)/shard_map/all_gather | solution.py:233
  168.1 0.8 fusion
  168.9 13.4 %all-to-all-done.4.parts_ref = bf16[64,32,256]{2,1,0:T(8,128)(2,1)S(1)} async-done(((bf16[64,32,256]{2,1,0:T(8,128)(2,1)}), bf16[64,32,256]{2,1,0:T(8,128)(2,1)S(1)}, u32[]{:S(2)}, u32[]{:S(2)}) %all-to-all-start.4) | async-done | bytes 1048608 | tf_op jit(solution)/shard_map/all_to_all | solution.py:231
  182.3 0.8 shard_map.134
  (1 shorter events, 0.0 us)
Async XLA Ops:
  0.6 46.0 %copy-start = (bf16[1,1,48,128,128]{4,3,2,1,0:T(8,128)(2,1)S(1)}, bf16[1,1,48,128,128]{4,3,2,1,0:T(8,128)(2,1)}, u32[]{:S(2)}) copy-start(bf16[1,1,48,128,128]{4,3,2,1,0:T(8,128)(2,1)} %vals_ref.3) | copy-start | bytes 4718596
  0.6 0.8 copy-start.6
  1.5 45.2 %copy-start.7 = (s32[1,1,48]{2,1,0:T(1,128)S(1)}, s32[1,1,48]{2,1,0:T(1,128)}, u32[]{:S(2)}) copy-start(s32[1,1,48]{2,1,0:T(1,128)} %rows_ref.3) | copy-start | bytes 580
  1.5 45.2 %copy-start.8 = (s32[1,1,48]{2,1,0:T(1,128)S(1)}, s32[1,1,48]{2,1,0:T(1,128)}, u32[]{:S(2)}) copy-start(s32[1,1,48]{2,1,0:T(1,128)} %cols_ref.3) | copy-start | bytes 580
  1.6 1.0 copy-start.1
  2.6 44.0 %all-to-all-start = ((bf16[64,32,256]{2,1,0:T(8,128)(2,1)}), bf16[64,32,256]{2,1,0:T(8,128)(2,1)S(1)}, u32[]{:S(2)}, u32[]{:S(2)}) async-start(bf16[64,32,256]{2,1,0:T(8,128)(2,1)} %copy-done.1), calls=%async_computation | async-start | bytes 2097152 | tf_op jit(solution)/shard_map/all_to_all | solution.py:200
  47.8 3.8 %collective-permute-start = (bf16[1024,256]{1,0:T(8,128)(2,1)S(1)}, bf16[1024,256]{1,0:T(8,128)(2,1)S(1)}, u32[]{:S(2)}, u32[]{:S(2)}) collective-permute-start(bf16[1024,256]{1,0:T(8,128)(2,1)S(1)} %get-tuple-element.12), channel_id=1, source_target_pairs={{0,1},{1,0},{2,3},{3,2},{4,5},{5,4},{6,7},{7,6},{8,9},{9,8},{10,11... | collective-permute-start | bytes 1572872 | tf_op jit(solution)/shard_map/ppermute | solution.py:210
  51.6 35.3 %copy-start.2 = (bf16[256,256]{1,0:T(8,128)(2,1)S(1)}, bf16[256,256]{1,0:T(8,128)(2,1)}, u32[]{:S(2)}) copy-start(bf16[256,256]{1,0:T(8,128)(2,1)} %w_neigh_ref.3) | copy-start | bytes 393220
  51.6 35.3 %copy-start.3 = (bf16[256,256]{1,0:T(8,128)(2,1)S(1)}, bf16[256,256]{1,0:T(8,128)(2,1)}, u32[]{:S(2)}) copy-start(bf16[256,256]{1,0:T(8,128)(2,1)} %w_self_ref.1) | copy-start | bytes 393220
  51.6 35.3 %copy-start.4 = (bf16[128,256]{1,0:T(8,128)(2,1)S(1)}, bf16[128,256]{1,0:T(8,128)(2,1)}, u32[]{:S(2)}) copy-start(bf16[128,256]{1,0:T(8,128)(2,1)} %own_ref.1) | copy-start | bytes 196612
  51.6 35.3 %copy-start.5 = (bf16[128,256]{1,0:T(8,128)(2,1)S(1)}, bf16[128,256]{1,0:T(8,128)(2,1)}, u32[]{:S(2)}) copy-start(bf16[128,256]{1,0:T(8,128)(2,1)} %cot_ref.1) | copy-start | bytes 196612
  88.0 26.6 %all-to-all-start.2 = ((bf16[16,64,128]{2,1,0:T(8,128)(2,1)}), bf16[16,64,128]{2,1,0:T(8,128)(2,1)S(1)}, u32[]{:S(2)}, u32[]{:S(2)}) async-start(bf16[16,64,128]{2,1,0:T(8,128)(2,1)} %get-tuple-element.16), calls=%async_computation.2 | async-start | bytes 524288 | tf_op jit(solution)/shard_map/all_to_all | solution.py:219
  130.7 14.0 %all-to-all-start.5 = ((f32[8,32,256]{2,1,0:T(8,128)}), f32[8,32,256]{2,1,0:T(8,128)S(1)}, u32[]{:S(2)}, u32[]{:S(2)}) async-start(f32[8,32,256]{2,1,0:T(8,128)} %shard_map.132.after_ref), calls=%async_computation.5 | async-start | bytes 524288 | tf_op jit(solution)/shard_map/all_to_all | solution.py:226
  144.8 37.5 %all-to-all-start.4 = ((bf16[64,32,256]{2,1,0:T(8,128)(2,1)}), bf16[64,32,256]{2,1,0:T(8,128)(2,1)S(1)}, u32[]{:S(2)}, u32[]{:S(2)}) async-start(bf16[64,32,256]{2,1,0:T(8,128)(2,1)} %bitcast.3), calls=%async_computation.4 | async-start | bytes 2097152 | tf_op jit(solution)/shard_map/all_to_all | solution.py:231

commit v7 on v6

--- a/solution.py
+++ b/solution.py
@@ -11,7 +11,7 @@
 GROUP = 16
 REST = 8
 SHARE = 16
-TAIL = 16
+TAIL = 8
 ROW = ("x", "y")
 COL = ("z", "core")
 F32 = jnp.float32

time: 184 us -> 182 us (0.989)
  blocking collectives: 89.3 us -> 87.4 us
where the time goes in v7:
time: 182 us
  blocking collectives  87.4 us (48%)
  waiting for transfers between devices  48 us (26%)
  starting transfers between devices  35.4 us (19%)
  Pallas kernels  5.69 us (3%)
  local copies, waits for them, and re-layouts  3.62 us (2%)
    all_to_all x1, blocking collectives, on_device(): parts = lax.all_to_all(pair, 'z', 0, 0, tiled=True)  34.4 us
    all_to_all x1, waiting for transfers between devices, on_device(): lax.all_to_all(repeat_rows(source_feats, n_row), ROW, 0, 0, tiled=True)  26 us
    all_gather x1, blocking collectives, on_device(): heads = lax.all_gather(head, COL, axis=0, tiled=True)  21.9 us
    all_to_all x1, starting transfers between devices, on_device(): lax.all_to_all(repeat_rows(source_feats, n_row), ROW, 0, 0, tiled=True)  17.3 us
    all_gather x1, blocking collectives, on_device(): all_grads = lax.all_gather(grads, COL, axis=0, tiled=False)  16 us
    all_to_all x1, blocking collectives, on_device(): grads = lax.all_to_all(grads, 'y', 0, 0, tiled=True)  15.1 us
    all_to_all x1, waiting for transfers between devices, on_device(): source_parts = lax.all_to_all(source_part, ROW, 0, 0, tiled=True)  13.4 us
    all_to_all x1, starting transfers between devices, on_device(): source_parts = lax.all_to_all(source_part, ROW, 0, 0, tiled=True)  7.23 us
  transfers between devices with their start and end apart: 5, of which 4 were waited for; matrix products, arithmetic and copies ran while one was open for 0% of the time, Pallas kernels for 1%

profile of v7, /device:TPU:4, one launch (start us, length us, event | category | flops | bytes accessed | tf_op | source)
XLA Modules:
  0.0 181.7 jit_solution(5635302586109806483)
XLA Ops:
  0.6 0.0 copy-start
  0.6 0.0 copy-start.7
  0.7 0.8 copy-done.7
  1.5 0.0 copy-start.8
  1.5 0.0 copy-start.9
  1.5 0.2 shard_map.128
  1.6 0.0 copy-start.2
  1.7 1.0 copy-done.2
  2.6 17.3 %all-to-all-start = ((bf16[64,32,256]{2,1,0:T(8,128)(2,1)}), bf16[64,32,256]{2,1,0:T(8,128)(2,1)S(1)}, u32[]{:S(2)}, u32[]{:S(2)}) async-start(bf16[64,32,256]{2,1,0:T(8,128)(2,1)} %copy-done.2), calls=%async_computation | async-start | bytes 2097152 | tf_op jit(solution)/shard_map/all_to_all | solution.py:200
  20.6 26.0 %all-to-all-done = bf16[64,32,256]{2,1,0:T(8,128)(2,1)S(1)} async-done(((bf16[64,32,256]{2,1,0:T(8,128)(2,1)}), bf16[64,32,256]{2,1,0:T(8,128)(2,1)S(1)}, u32[]{:S(2)}, u32[]{:S(2)}) %all-to-all-start) | async-done | bytes 1048608 | tf_op jit(solution)/shard_map/all_to_all | solution.py:200
  46.7 0.0 copy-done
  46.7 0.0 copy-done.8
  46.7 0.0 copy-done.9
  46.7 1.1 shard_map.129
  47.8 1.9 %collective-permute-start = (bf16[1024,256]{1,0:T(8,128)(2,1)S(1)}, bf16[1024,256]{1,0:T(8,128)(2,1)S(1)}, u32[]{:S(2)}, u32[]{:S(2)}) collective-permute-start(bf16[1024,256]{1,0:T(8,128)(2,1)S(1)} %get-tuple-element.12), channel_id=1, source_target_pairs={{0,1},{1,0},{2,3},{3,2},{4,5},{5,4},{6,7},{7,6},{8,9},{9,8},{10,11... | collective-permute-start | bytes 1572872 | tf_op jit(solution)/shard_map/ppermute | solution.py:210
  49.7 1.9 %collective-permute-done = bf16[1024,256]{1,0:T(8,128)(2,1)S(1)} collective-permute-done((bf16[1024,256]{1,0:T(8,128)(2,1)S(1)}, bf16[1024,256]{1,0:T(8,128)(2,1)S(1)}, u32[]{:S(2)}, u32[]{:S(2)}) %collective-permute-start) | collective-permute-done | bytes 524320 | tf_op jit(solution)/shard_map/ppermute | solution.py:210
  51.6 0.0 copy-start.3
  51.6 0.0 copy-start.4
  51.6 0.0 copy-start.5
  51.6 0.0 copy-start.6
  51.6 0.1 add_convert_fusion
  51.7 34.4 %all_to_all.38.parts_ref = bf16[8,128,256]{2,1,0:T(8,128)(2,1)S(1)} all-to-all(bf16[8,128,256]{2,1,0:T(8,128)(2,1)S(1)} %bitcast.12), channel_id=1, replica_groups=mesh['x'=8,'y'=8,'z'=8,'core'=2] {'z'}, dimensions={0} | all-to-all | bytes 1048576 | tf_op jit(solution)/shard_map/all_to_all | solution.py:212
  86.1 0.0 copy-done.3
  86.1 0.0 copy-done.4
  86.2 0.0 copy-done.5
  86.2 0.0 copy-done.6
  86.2 1.1 shard_map.130
  87.3 3.5 %all-to-all-start.2 = ((bf16[16,48,128]{2,1,0:T(8,128)(2,1)}), bf16[16,48,128]{2,1,0:T(8,128)(2,1)S(1)}, u32[]{:S(2)}, u32[]{:S(2)}) async-start(bf16[16,48,128]{2,1,0:T(8,128)(2,1)} %get-tuple-element.16), calls=%async_computation.2 | async-start | bytes 393216 | tf_op jit(solution)/shard_map/all_to_all | solution.py:219
  90.8 21.9 %all_gather.9.head_ref = bf16[1920,256]{1,0:T(8,128)(2,1)S(1)} all-gather(bf16[120,256]{1,0:T(8,128)(2,1)S(1)} %get-tuple-element.15), channel_id=1, replica_groups=mesh['x'=8,'y'=8,'z'=8,'core'=2] {'z','core'}, dimensions={0}, use_global_device_ids=true | all-gather | bytes 1044480 | tf_op jit(solution)/shard_map/all_gather | solution.py:220
  112.7 0.0 all-to-all-done.2.swap_ref
  112.7 0.3 shard_map.131
  113.0 15.1 %all_to_all.39.parts_ref = f32[8,32,256]{2,1,0:T(8,128)S(1)} all-to-all(f32[8,32,256]{2,1,0:T(8,128)S(1)} %shard_map.131), channel_id=1, replica_groups=mesh['x'=8,'y'=8,'z'=8,'core'=2] {'y'}, dimensions={0} | all-to-all | bytes 524288 | tf_op jit(solution)/shard_map/all_to_all | solution.py:224
  128.1 0.7 shard_map.132.after_ref
  128.8 5.4 %all-to-all-start.5 = ((f32[8,32,256]{2,1,0:T(8,128)}), f32[8,32,256]{2,1,0:T(8,128)S(1)}, u32[]{:S(2)}, u32[]{:S(2)}) async-start(f32[8,32,256]{2,1,0:T(8,128)} %shard_map.132.after_ref), calls=%async_computation.5 | async-start | bytes 524288 | tf_op jit(solution)/shard_map/all_to_all | solution.py:226
  134.2 1.5 shard_map.133
  135.7 0.0 copy-start.1
  135.7 1.0 copy-done.1
  136.7 6.7 %all-to-all-done.5 = f32[8,32,256]{2,1,0:T(8,128)S(1)} async-done(((f32[8,32,256]{2,1,0:T(8,128)}), f32[8,32,256]{2,1,0:T(8,128)S(1)}, u32[]{:S(2)}, u32[]{:S(2)}) %all-to-all-start.5) | async-done | bytes 262176 | tf_op jit(solution)/shard_map/all_to_all | solution.py:226
  143.4 7.2 %all-to-all-start.4 = ((bf16[64,32,256]{2,1,0:T(8,128)(2,1)}), bf16[64,32,256]{2,1,0:T(8,128)(2,1)S(1)}, u32[]{:S(2)}, u32[]{:S(2)}) async-start(bf16[64,32,256]{2,1,0:T(8,128)(2,1)} %bitcast.9), calls=%async_computation.4 | async-start | bytes 2097152 | tf_op jit(solution)/shard_map/all_to_all | solution.py:231
  150.7 16.0 %all-gather = f32[512,256]{1,0:T(8,128)S(1)} all-gather(f32[32,256]{1,0:T(8,128)S(1)} %reduce_sum.9), channel_id=2, replica_groups=mesh['x'=8,'y'=8,'z'=8,'core'=2] {'z','core'}, dimensions={0}, use_global_device_ids=true | all-gather | bytes 557056 | tf_op jit(solution)/shard_map/all_gather | solution.py:233
  166.7 0.8 fusion
  167.6 13.4 %all-to-all-done.4.parts_ref = bf16[64,32,256]{2,1,0:T(8,128)(2,1)S(1)} async-done(((bf16[64,32,256]{2,1,0:T(8,128)(2,1)}), bf16[64,32,256]{2,1,0:T(8,128)(2,1)S(1)}, u32[]{:S(2)}, u32[]{:S(2)}) %all-to-all-start.4) | async-done | bytes 1048608 | tf_op jit(solution)/shard_map/all_to_all | solution.py:231
  180.9 0.8 shard_map.134
  (1 shorter events, 0.0 us)
Async XLA Ops:
  0.6 46.0 %copy-start = (bf16[1,1,48,128,128]{4,3,2,1,0:T(8,128)(2,1)S(1)}, bf16[1,1,48,128,128]{4,3,2,1,0:T(8,128)(2,1)}, u32[]{:S(2)}) copy-start(bf16[1,1,48,128,128]{4,3,2,1,0:T(8,128)(2,1)} %vals_ref.3) | copy-start | bytes 4718596
  0.6 0.8 copy-start.7
  1.5 45.2 %copy-start.8 = (s32[1,1,48]{2,1,0:T(1,128)S(1)}, s32[1,1,48]{2,1,0:T(1,128)}, u32[]{:S(2)}) copy-start(s32[1,1,48]{2,1,0:T(1,128)} %rows_ref.3) | copy-start | bytes 580
  1.5 45.2 %copy-start.9 = (s32[1,1,48]{2,1,0:T(1,128)S(1)}, s32[1,1,48]{2,1,0:T(1,128)}, u32[]{:S(2)}) copy-start(s32[1,1,48]{2,1,0:T(1,128)} %cols_ref.3) | copy-start | bytes 580
  1.6 1.0 copy-start.2
  2.6 44.0 %all-to-all-start = ((bf16[64,32,256]{2,1,0:T(8,128)(2,1)}), bf16[64,32,256]{2,1,0:T(8,128)(2,1)S(1)}, u32[]{:S(2)}, u32[]{:S(2)}) async-start(bf16[64,32,256]{2,1,0:T(8,128)(2,1)} %copy-done.2), calls=%async_computation | async-start | bytes 2097152 | tf_op jit(solution)/shard_map/all_to_all | solution.py:200
  47.8 3.8 %collective-permute-start = (bf16[1024,256]{1,0:T(8,128)(2,1)S(1)}, bf16[1024,256]{1,0:T(8,128)(2,1)S(1)}, u32[]{:S(2)}, u32[]{:S(2)}) collective-permute-start(bf16[1024,256]{1,0:T(8,128)(2,1)S(1)} %get-tuple-element.12), channel_id=1, source_target_pairs={{0,1},{1,0},{2,3},{3,2},{4,5},{5,4},{6,7},{7,6},{8,9},{9,8},{10,11... | collective-permute-start | bytes 1572872 | tf_op jit(solution)/shard_map/ppermute | solution.py:210
  51.6 34.5 %copy-start.3 = (bf16[256,256]{1,0:T(8,128)(2,1)S(1)}, bf16[256,256]{1,0:T(8,128)(2,1)}, u32[]{:S(2)}) copy-start(bf16[256,256]{1,0:T(8,128)(2,1)} %w_neigh_ref.3) | copy-start | bytes 393220
  51.6 34.5 %copy-start.4 = (bf16[256,256]{1,0:T(8,128)(2,1)S(1)}, bf16[256,256]{1,0:T(8,128)(2,1)}, u32[]{:S(2)}) copy-start(bf16[256,256]{1,0:T(8,128)(2,1)} %w_self_ref.1) | copy-start | bytes 393220
  51.6 34.5 %copy-start.5 = (bf16[128,256]{1,0:T(8,128)(2,1)S(1)}, bf16[128,256]{1,0:T(8,128)(2,1)}, u32[]{:S(2)}) copy-start(bf16[128,256]{1,0:T(8,128)(2,1)} %own_ref.1) | copy-start | bytes 196612
  51.6 34.5 %copy-start.6 = (bf16[128,256]{1,0:T(8,128)(2,1)S(1)}, bf16[128,256]{1,0:T(8,128)(2,1)}, u32[]{:S(2)}) copy-start(bf16[128,256]{1,0:T(8,128)(2,1)} %cot_ref.1) | copy-start | bytes 196612
  87.3 25.5 %all-to-all-start.2 = ((bf16[16,48,128]{2,1,0:T(8,128)(2,1)}), bf16[16,48,128]{2,1,0:T(8,128)(2,1)S(1)}, u32[]{:S(2)}, u32[]{:S(2)}) async-start(bf16[16,48,128]{2,1,0:T(8,128)(2,1)} %get-tuple-element.16), calls=%async_computation.2 | async-start | bytes 393216 | tf_op jit(solution)/shard_map/all_to_all | solution.py:219
  128.8 14.6 %all-to-all-start.5 = ((f32[8,32,256]{2,1,0:T(8,128)}), f32[8,32,256]{2,1,0:T(8,128)S(1)}, u32[]{:S(2)}, u32[]{:S(2)}) async-start(f32[8,32,256]{2,1,0:T(8,128)} %shard_map.132.after_ref), calls=%async_computation.5 | async-start | bytes 524288 | tf_op jit(solution)/shard_map/all_to_all | solution.py:226
  135.7 1.0 copy-start.1
  143.4 37.5 %all-to-all-start.4 = ((bf16[64,32,256]{2,1,0:T(8,128)(2,1)}), bf16[64,32,256]{2,1,0:T(8,128)(2,1)S(1)}, u32[]{:S(2)}, u32[]{:S(2)}) async-start(bf16[64,32,256]{2,1,0:T(8,128)(2,1)} %bitcast.9), calls=%async_computation.4 | async-start | bytes 2097152 | tf_op jit(solution)/shard_map/all_to_all | solution.py:231
